TPU v7x, 32 devices: a whole 2x2x4 slice. The times are simulated.
32 devices in a mesh: tm: 16 (over z, y, x), head: 2 (over core).
Axes of the slice: x: 2, y: 2, z: 4, core: 2. Of those that a mesh axis runs over, the one named last changes fastest.
Arguments:
- clean_qkv: bfloat16 [3, 8192, 5120], P(None, 'tm', 'head'), may hold values from -140 to 140
- noise_qkv: bfloat16 [3, 8192, 5120], P(None, 'tm', 'head'), may hold values from -140 to 140
- timestep: int32 [16], P('tm'), may hold values from 1 to 999
- gain_q: float32 [5120], P('head'), may hold values from 0.1 to 1.9
- gain_k: float32 [5120], P('head'), may hold values from 0.1 to 1.9
- attended_grad: bfloat16 [8192, 5120], P('tm', 'head'), may hold values from -6 to 6
Outputs:
- attended: bfloat16 [8192, 5120], P('tm', 'head')
- clean_grads: float32 [3, 8192, 5120], P(None, 'tm', 'head')
All inputs are finite; a program needn't handle non-finite values.
Results may differ from a plain program's by a relative error of at most 0.012.
The roundings to bfloat16 on the way count: a program that leaves them out, or rounds other values in their place, can miss the bound.
Values may be sent and summed in bfloat16 or wider, within the bound.
A program may use at most 256 MiB of HBM per device.

v0:
```python
import jax
import jax.numpy as jnp
from jax import lax
from jax.sharding import PartitionSpec as P

D = 5120
HEAD_DIM = 128
CONTEXT = 3


epsilon = 1e-06
masked_score = -1e30


def from_behind(block, axis, distance):
    devices = range(lax.axis_size(axis))
    route = [(i - distance, i) for i in devices if i - distance in devices]
    return lax.ppermute(block, axis, route)


def noise_share_of(timestep):
    level = timestep.astype(jnp.float32) / 1000.0
    return 5.0 * level / (1.0 + 4.0 * level)


def contract(left, right, left_dim, right_dim):
    return lax.dot_general(
        left, right, (((left_dim,), (right_dim,)), ((), ())), preferred_element_type=jnp.float32
    )


def on_device(clean_qkv, noise_qkv, timestep, gain_q, gain_k, attended_grad):
    row_count = clean_qkv.shape[1]
    local_width = clean_qkv.shape[2]
    heads_here = local_width // HEAD_DIM
    span_index = lax.axis_index("tm")
    noise_share = noise_share_of(timestep[0])
    keep_share = 1.0 - noise_share
    clean_field = clean_qkv.astype(jnp.float32)
    noisy_field = keep_share * clean_field + noise_share * noise_qkv.astype(jnp.float32)
    partial_sums = jnp.stack(
        [
            jnp.sum(noisy_field[0] * noisy_field[0], axis=-1),
            jnp.sum(noisy_field[1] * noisy_field[1], axis=-1),
            jnp.sum(clean_field[1] * clean_field[1], axis=-1),
        ]
    )
    totals = lax.psum(partial_sums, "head")
    inverse = lax.rsqrt(totals / D + epsilon)
    query_rows = (noisy_field[0] * inverse[0][:, None] * gain_q).astype(jnp.bfloat16)
    key_own = (noisy_field[1] * inverse[1][:, None] * gain_k).astype(jnp.bfloat16)
    key_clean = (clean_field[1] * inverse[2][:, None] * gain_k).astype(jnp.bfloat16)
    value_own = noisy_field[2].astype(jnp.bfloat16)
    value_clean = clean_qkv[2]
    outgoing = jnp.stack([key_clean, value_clean])
    arrived = []
    for hop_index in range(CONTEXT):
        arrived.append(from_behind(outgoing, "tm", hop_index + 1))
    key_rows = jnp.concatenate([key_own] + [piece[0] for piece in arrived], axis=0)
    value_rows = jnp.concatenate([value_own] + [piece[1] for piece in arrived], axis=0)
    block_ids = jnp.arange(CONTEXT + 1, dtype=jnp.int32)
    block_valid = span_index >= block_ids
    key_valid = jnp.repeat(block_valid, row_count)
    score_scale = HEAD_DIM ** (-0.5)
    key_count = (CONTEXT + 1) * row_count

    def one_head(head_index, carried_state):
        output_acc, query_acc, keys_acc, values_acc, stat_acc = carried_state
        head_start = head_index * HEAD_DIM
        query_head = lax.dynamic_slice_in_dim(query_rows, head_start, HEAD_DIM, 1)
        key_head = lax.dynamic_slice_in_dim(key_rows, head_start, HEAD_DIM, 1)
        value_head = lax.dynamic_slice_in_dim(value_rows, head_start, HEAD_DIM, 1)
        grad_head = lax.dynamic_slice_in_dim(attended_grad, head_start, HEAD_DIM, 1)
        scores = contract(query_head, key_head, 1, 1) * score_scale
        scores = jnp.where(key_valid[None, :], scores, masked_score)
        row_max = jnp.max(scores, axis=-1, keepdims=True)
        exponent = jnp.exp(scores - row_max)
        row_total = jnp.sum(exponent, axis=-1, keepdims=True)
        attention = exponent / row_total
        weights = attention.astype(jnp.bfloat16)
        output_head = jnp.dot(weights, value_head, preferred_element_type=jnp.float32)
        grad_probs = contract(grad_head, value_head, 1, 1)
        row_delta = jnp.sum(attention * grad_probs, axis=-1, keepdims=True)
        grad_scores = (attention * (grad_probs - row_delta) * score_scale).astype(jnp.bfloat16)
        grad_query_head = jnp.dot(grad_scores, key_head, preferred_element_type=jnp.float32)
        grad_key_head = contract(grad_scores, query_head, 0, 0)
        grad_value_head = contract(weights, grad_head, 0, 0)
        head_stats = jnp.stack([row_max[:, 0], row_total[:, 0], row_delta[:, 0]])[:, None, :]
        output_acc = lax.dynamic_update_slice_in_dim(output_acc, output_head, head_start, 1)
        query_acc = lax.dynamic_update_slice_in_dim(query_acc, grad_query_head, head_start, 1)
        keys_acc = lax.dynamic_update_slice_in_dim(keys_acc, grad_key_head, head_start, 1)
        values_acc = lax.dynamic_update_slice_in_dim(values_acc, grad_value_head, head_start, 1)
        stat_acc = lax.dynamic_update_slice_in_dim(stat_acc, head_stats, head_index, 1)
        return (output_acc, query_acc, keys_acc, values_acc, stat_acc)

    start_state = (
        jnp.zeros((row_count, local_width), jnp.float32),
        jnp.zeros((row_count, local_width), jnp.float32),
        jnp.zeros((key_count, local_width), jnp.float32),
        jnp.zeros((key_count, local_width), jnp.float32),
        jnp.zeros((3, heads_here, row_count), jnp.float32),
    )
    output_acc, grad_query, grad_keys, grad_values, row_stats = lax.fori_loop(
        0, heads_here, one_head, start_state
    )
    attended = output_acc.astype(jnp.bfloat16)
    returns_parts = []
    for hop_index in range(1, CONTEXT + 1):
        lower = hop_index * row_count
        returns_parts.append(
            jnp.stack(
                [grad_keys[lower : lower + row_count], grad_values[lower : lower + row_count]]
            )
        )
    context_grads = jnp.zeros_like(returns_parts[0])
    for hop_index in range(CONTEXT):
        context_grads = context_grads + from_behind(
            returns_parts[hop_index], "tm", -(hop_index + 1)
        )
    context_key_grad = context_grads[0]
    context_value_grad = context_grads[1]
    own_key_grad = grad_keys[:row_count]
    inner_sums = jnp.stack(
        [
            jnp.sum(noisy_field[0] * gain_q * grad_query, axis=-1),
            jnp.sum(noisy_field[1] * gain_k * own_key_grad, axis=-1),
            jnp.sum(clean_field[1] * gain_k * context_key_grad, axis=-1),
        ]
    )
    inner_totals = lax.psum(inner_sums, "head")
    cube_term = inverse**3 * inner_totals / D
    grad_query_pre = (
        inverse[0][:, None] * gain_q * grad_query - noisy_field[0] * cube_term[0][:, None]
    )
    grad_own_pre = (
        inverse[1][:, None] * gain_k * own_key_grad - noisy_field[1] * cube_term[1][:, None]
    )
    grad_clean_pre = (
        inverse[2][:, None] * gain_k * context_key_grad - clean_field[1] * cube_term[2][:, None]
    )
    clean_grads = jnp.stack(
        [
            keep_share * grad_query_pre,
            keep_share * grad_own_pre + grad_clean_pre,
            keep_share * grad_values[:row_count] + context_value_grad,
        ]
    )
    return (attended, clean_grads)


def solution(mesh):
    placed = (
        P(None, "tm", "head"),
        P(None, "tm", "head"),
        P("tm"),
        P("head"),
        P("head"),
        P("tm", "head"),
    )
    return jax.shard_map(
        on_device,
        mesh=mesh,
        in_specs=placed,
        out_specs=(P("tm", "head"), P(None, "tm", "head")),
        check_vma=False,
    )
```

profile of v0, /device:TPU:5, one launch (start us, length us, event | category | flops | bytes accessed | tf_op | source)
XLA Modules:
  0.0 1671.7 jit_solution(8187640571765377832)
XLA Ops:
  0.6 10.9 convert_element_type.42
  12.2 14.3 multiply_add_fusion
  26.4 4.8 multiply_reduce_fusion.4
  43.5 6.6 collective-permute-start.2
  58.6 5.8 multiply_convert_fusion.2
  64.4 95.8 %collective-permute-done.2 = bf16[2,512,2560]{2,1,0:T(8,128)(2,1)} collective-permute-done((bf16[2,512,2560]{2,1,0:T(8,128)(2,1)}, bf16[2,512,2560]{2,1,0:T(8,128)(2,1)}, u32[]{:S(2)}, u32[]{:S(2)}) %collective-permute-start.2) | collective-permute-done | bytes 5242912 | tf_op jit(solution)/shard_map/ppermute | solution.py:18
  163.0 115.6 %collective-permute-done.1 = bf16[2,512,2560]{2,1,0:T(8,128)(2,1)} collective-permute-done((bf16[2,512,2560]{2,1,0:T(8,128)(2,1)}, bf16[2,512,2560]{2,1,0:T(8,128)(2,1)}, u32[]{:S(2)}, u32[]{:S(2)}) %collective-permute-start.1) | collective-permute-done | bytes 5242912 | tf_op jit(solution)/shard_map/ppermute | solution.py:18
  284.4 7.6 pad_maximum_fusion.1
  294.9 9.6 broadcast.33.clone
  304.6 9.6 broadcast.33
  314.2 361.6 %while.20 = (s32[]{:T(128)}, bf16[512,2560]{1,0:T(8,128)(2,1)S(1)}, f32[512,2560]{1,0:T(8,128)}, f32[2048,2560]{1,0:T(8,128)}, f32[2048,2560]{1,0:T(8,128)}, /*i...) while((s32[]{:T(128)}, bf16[512,2560]{1,0:T(8,128)(2,1)S(1)}, ...), condition=%wide.region_8.9_spmd.clone, body=%wide.region_4.8_spmd.clone.sunk | while | flops 1643117056 | bytes 45140152 | solution.py:103
  675.8 12.3 slice_bitcast_fusion.6
  688.2 11.5 slice_bitcast_fusion.7
  699.6 9.8 pad_maximum_fusion.5
  710.7 4.7 pad_maximum_fusion.3
  717.7 10.1 pad_maximum_fusion.4
  730.1 208.7 %collective-permute-done.5 = f32[2,512,2560]{2,1,0:T(8,128)} collective-permute-done((f32[2,512,2560]{2,1,0:T(8,128)}, f32[2,512,2560]{2,1,0:T(8,128)}, u32[]{:S(2)}, u32[]{:S(2)}) %collective-permute-start.5) | collective-permute-done | bytes 10485792 | tf_op jit(solution)/shard_map/ppermute | solution.py:18
  938.9 326.7 %collective-permute-done.3 = f32[2,512,2560]{2,1,0:T(8,128)} collective-permute-done((f32[2,512,2560]{2,1,0:T(8,128)}, f32[2,512,2560]{2,1,0:T(8,128)}, u32[]{:S(2)}, u32[]{:S(2)}) %collective-permute-start.3) | collective-permute-done | bytes 10485792 | tf_op jit(solution)/shard_map/ppermute | solution.py:18
  1265.5 347.1 %collective-permute-done.4 = f32[2,512,2560]{2,1,0:T(8,128)} collective-permute-done((f32[2,512,2560]{2,1,0:T(8,128)}, f32[2,512,2560]{2,1,0:T(8,128)}, u32[]{:S(2)}, u32[]{:S(2)}) %collective-permute-start.4) | collective-permute-done | bytes 10485792 | tf_op jit(solution)/shard_map/ppermute | solution.py:18
  1612.6 15.6 add_add_fusion
  1628.2 7.1 multiply_reduce_fusion.2
  1636.1 4.0 psum.15
  1640.1 20.5 %multiply_bitcast_fusion = (f32[1,512,2560]{2,1,0:T(8,128)}, f32[1,512,2560]{2,1,0:T(8,128)}, f32[1,512,2560]{2,1,0:T(8,128)}) fusion(f32[512,2560]{1,0:T(8,128)} %get-tuple-element.175, f32[3,512,2560]{2,1,0:T(8,128)} %multiply_add_fusion, f32[512]{0:T(512)S(1)} %bitcast.128, f32[]{:T(128)S(6)} %sub.52, f32[2560]{0:T(1024)S(1)} %copy-done.7, ...), kind=kLoop, calls=%fused_computation.56 | loop fusion | flops 22282240 | bytes 57704452 | tf_op jit(solution)/shard_map/stack | solution.py:141
  1660.6 11.1 pad_maximum_fusion
  (269 shorter events, 400.2 us)
Async XLA Ops:
  37.2 21.4 %copy-start.10 = (f32[1,512]{1,0:T(1,128)}, f32[1,512]{1,0:T(1,128)S(1)}, u32[]{:S(2)}) copy-start(f32[1,512]{1,0:T(1,128)S(1)} %get-tuple-element.250) | copy-start | bytes 6148
  37.2 21.4 %copy-start.14 = (f32[1,512]{1,0:T(1,128)}, f32[1,512]{1,0:T(1,128)S(1)}, u32[]{:S(2)}) copy-start(f32[1,512]{1,0:T(1,128)S(1)} %get-tuple-element.252) | copy-start | bytes 6148
  43.5 15.1 copy-start.6
  43.5 116.6 %collective-permute-start.2 = (bf16[2,512,2560]{2,1,0:T(8,128)(2,1)}, bf16[2,512,2560]{2,1,0:T(8,128)(2,1)}, u32[]{:S(2)}, u32[]{:S(2)}) collective-permute-start(bf16[2,512,2560]{2,1,0:T(8,128)(2,1)} %pad_maximum_fusion.6), channel_id=1, source_target_pairs={{0,6},{2,8},{4,10},{6,12},{8,14},{10,16},{12,18},{14,20},{16,22},{... | collective-permute-start | bytes 15728648 | tf_op jit(solution)/shard_map/ppermute | solution.py:18
  50.1 228.5 %collective-permute-start.1 = (bf16[2,512,2560]{2,1,0:T(8,128)(2,1)}, bf16[2,512,2560]{2,1,0:T(8,128)(2,1)}, u32[]{:S(2)}, u32[]{:S(2)}) collective-permute-start(bf16[2,512,2560]{2,1,0:T(8,128)(2,1)} %pad_maximum_fusion.6), channel_id=1, source_target_pairs={{0,4},{2,6},{4,8},{6,10},{8,12},{10,14},{12,16},{14,18},{16,20},{1... | collective-permute-start | bytes 15728648 | tf_op jit(solution)/shard_map/ppermute | solution.py:18
  52.0 229.5 %collective-permute-start = (bf16[2,512,2560]{2,1,0:T(8,128)(2,1)}, bf16[2,512,2560]{2,1,0:T(8,128)(2,1)}, u32[]{:S(2)}, u32[]{:S(2)}) collective-permute-start(bf16[2,512,2560]{2,1,0:T(8,128)(2,1)} %pad_maximum_fusion.6), channel_id=1, source_target_pairs={{0,2},{2,4},{4,6},{6,8},{8,10},{10,12},{12,14},{14,16},{16,18},{18... | collective-permute-start | bytes 15728648 | tf_op jit(solution)/shard_map/ppermute | solution.py:18
  304.6 9.6 copy-start.2
  675.8 12.3 copy-start.3
  699.6 11.1 copy-start
  699.6 11.1 copy-start.1
  709.4 229.4 %collective-permute-start.5 = (f32[2,512,2560]{2,1,0:T(8,128)}, f32[2,512,2560]{2,1,0:T(8,128)}, u32[]{:S(2)}, u32[]{:S(2)}) collective-permute-start(f32[2,512,2560]{2,1,0:T(8,128)} %pad_maximum_fusion.5), channel_id=1, source_target_pairs={{6,0},{8,2},{10,4},{12,6},{14,8},{16,10},{18,12},{20,14},{22,16},{... | collective-permute-start | bytes 31457288 | tf_op jit(solution)/shard_map/ppermute | solution.py:18
  715.5 550.1 %collective-permute-start.3 = (f32[2,512,2560]{2,1,0:T(8,128)}, f32[2,512,2560]{2,1,0:T(8,128)}, u32[]{:S(2)}, u32[]{:S(2)}) collective-permute-start(f32[2,512,2560]{2,1,0:T(8,128)} %pad_maximum_fusion.3), channel_id=1, source_target_pairs={{2,0},{4,2},{6,4},{8,6},{10,8},{12,10},{14,12},{16,14},{18,16},{20... | collective-permute-start | bytes 31457288 | tf_op jit(solution)/shard_map/ppermute | solution.py:18
  717.6 910.5 %slice-start = ((s8[15728640]{0:T(1024)(128)(4,1)}), s8[4194304]{0:T(1024)(128)(4,1)S(1)}, s32[]{:S(2)}) async-start(s8[15728640]{0:T(1024)(128)(4,1)} %bitcast.106), calls=%async_computation | async-start | bytes 8388608
  717.6 910.5 %slice-start.1 = ((s8[15728640]{0:T(1024)(128)(4,1)}), s8[3145728]{0:T(1024)(128)(4,1)S(1)}, s32[]{:S(2)}) async-start(s8[15728640]{0:T(1024)(128)(4,1)} %bitcast.106), calls=%async_computation.1 | async-start | bytes 6291456
  717.7 910.5 %slice-start.4 = ((s8[5242880]{0:T(1024)(128)(4,1)}), s8[4194304]{0:T(1024)(128)(4,1)S(1)}, s32[]{:S(2)}) async-start(s8[5242880]{0:T(1024)(128)(4,1)} %bitcast.108), calls=%async_computation.4 | async-start | bytes 8388608
  727.8 900.4 %slice-start.2 = ((s8[15728640]{0:T(1024)(128)(4,1)}), s8[4194304]{0:T(1024)(128)(4,1)S(1)}, s32[]{:S(2)}) async-start(s8[15728640]{0:T(1024)(128)(4,1)} %bitcast.106), calls=%async_computation.2 | async-start | bytes 8388608
  727.8 900.4 %slice-start.3 = ((s8[15728640]{0:T(1024)(128)(4,1)}), s8[4194304]{0:T(1024)(128)(4,1)S(1)}, s32[]{:S(2)}) async-start(s8[15728640]{0:T(1024)(128)(4,1)} %bitcast.106), calls=%async_computation.3 | async-start | bytes 8388608
  727.8 900.4 %slice-start.5 = ((s8[5242880]{0:T(1024)(128)(4,1)}), s8[1048576]{0:T(1024)(128)(4,1)S(1)}, s32[]{:S(2)}) async-start(s8[5242880]{0:T(1024)(128)(4,1)} %bitcast.108), calls=%async_computation.5 | async-start | bytes 2097152
  727.8 900.4 %copy-start.5 = (f32[2560]{0:T(1024)S(1)}, f32[2560]{0:T(1024)}, u32[]{:S(2)}) copy-start(f32[2560]{0:T(1024)} %param.12) | copy-start | bytes 30724
  727.8 900.4 %copy-start.7 = (f32[2560]{0:T(1024)S(1)}, f32[2560]{0:T(1024)}, u32[]{:S(2)}) copy-start(f32[2560]{0:T(1024)} %param.11) | copy-start | bytes 30724
  727.8 884.8 %collective-permute-start.4 = (f32[2,512,2560]{2,1,0:T(8,128)}, f32[2,512,2560]{2,1,0:T(8,128)}, u32[]{:S(2)}, u32[]{:S(2)}) collective-permute-start(f32[2,512,2560]{2,1,0:T(8,128)} %pad_maximum_fusion.4), channel_id=1, source_target_pairs={{4,0},{6,2},{8,4},{10,6},{12,8},{14,10},{16,12},{18,14},{20,16},{2... | collective-permute-start | bytes 31457288 | tf_op jit(solution)/shard_map/ppermute | solution.py:18
  1628.2 11.8 copy-start.9
  1628.2 11.8 copy-start.11
  1628.2 11.8 copy-start.13
  (4 other events, 20.1 us)
where the time goes:
time: 1680 us; the launch traced here: 1670 us
  waiting for transfers between devices  1090 us (65%)
  matrix products  307 us (18%)
  other arithmetic  186 us (11%)
  local copies, waits for them, and re-layouts  59.8 us (4%)
    ppermute x6, waiting for transfers between devices, from_behind(): return lax.ppermute(block, axis, route)  1090 us
    dot_general x80, matrix products, contract(): lax.dot_general(left, right, (((left_dim,), (right_dim,)), ((), ())), pre...  212 us
    dot_general x20, matrix products, one_head(): jnp.dot(grad_scores, key_head, preferred_element_type=jnp.float32)  50.2 us
    dot_general x20, matrix products, one_head(): jnp.dot(weights, value_head, preferred_element_type=jnp.float32)  44.7 us
    convert_element_type x20, other arithmetic, one_head(): (attention * (grad_probs - row_delta) * score_scale).astype(jnp.bfloat16)  33.7 us
  transfers between devices with their start and end apart: 6, of which 5 were waited for; matrix products, arithmetic and copies ran while one was open for 2% of the time, Pallas kernels for 0%

commit v1 on v0

--- a/solution.py
+++ b/solution.py
@@ -1,6 +1,9 @@
+import functools
 import jax
 import jax.numpy as jnp
 from jax import lax
+from jax.experimental import pallas as pl
+from jax.experimental.pallas import tpu as pltpu
 from jax.sharding import PartitionSpec as P
 
 D = 5120
@@ -148,6 +151,334 @@
     return (attended, clean_grads)
 
 
+GROUP = 4
+ROWS = 64
+LOG2E = 1.4426950408889634
+VMEM_LIMIT = 52 * 1024 * 1024
+
+
+def chunks_of(heads):
+    sizes = []
+    while heads > 0:
+        sizes.append(min(2, heads))
+        heads -= sizes[-1]
+    return sizes
+
+
+def swap(block, distance):
+    return lax.ppermute(block, "tm", [(i, i ^ distance) for i in range(lax.axis_size("tm"))])
+
+
+def other_core(block):
+    return lax.ppermute(block, "head", [(0, 1), (1, 0)])
+
+
+def columns_at(place, width, offset, count):
+    return pl.ds(pl.multiple_of(place * width + offset, HEAD_DIM), count)
+
+
+def pack_lanes(parts):
+    lane = lax.broadcasted_iota(jnp.int32, (parts[0].shape[0], 128), 1)
+    packed = jnp.zeros((parts[0].shape[0], 128), jnp.float32)
+    for index, part in enumerate(parts):
+        packed = jnp.where(lane == index, part, packed)
+    return packed
+
+
+def values_kernel(width, place_ref, share_ref, clean_ref, noise_ref, grad_ref, sums_ref, *out_refs):
+    keep, share = share_ref[0], share_ref[1]
+    place = place_ref[0]
+    squares = [0.0, 0.0, 0.0]
+    for group in range(GROUP):
+        cols = pl.ds(group * width, width)
+        clean_key = clean_ref[1, :, cols].astype(jnp.float32)
+        query = keep * clean_ref[0, :, cols].astype(jnp.float32) + share * noise_ref[0, :, cols].astype(jnp.float32)
+        key = keep * clean_key + share * noise_ref[1, :, cols].astype(jnp.float32)
+        for index, field in enumerate((query, key, clean_key)):
+            squares[index] = squares[index] + jnp.sum(field * field, axis=-1, keepdims=True)
+    sums_ref[...] = pack_lanes(squares)
+    for distance in range(GROUP):
+        cols = columns_at(place ^ distance, width, 0, width)
+        clean = clean_ref[2, :, cols]
+        noisy = keep * clean.astype(jnp.float32) + share * noise_ref[2, :, cols].astype(jnp.float32)
+        out_refs[distance][0] = clean
+        out_refs[distance][1] = noisy.astype(jnp.bfloat16)
+        out_refs[distance][2] = grad_ref[:, cols]
+
+
+def keys_kernel(width, sizes, place_ref, share_ref, clean_ref, noise_ref, gains_ref, sums_ref, other_ref, *out_refs):
+    keep, share = share_ref[0], share_ref[1]
+    place = place_ref[0]
+    inverse = lax.rsqrt((sums_ref[...] + other_ref[...]) / D + epsilon)
+    for distance in range(GROUP):
+        offset = 0
+        for chunk, heads in enumerate(sizes):
+            count = heads * HEAD_DIM
+            cols = columns_at(place ^ distance, width, offset, count)
+            out_ref = out_refs[chunk * GROUP + distance]
+            gain_q, gain_k = gains_ref[0:1, cols], gains_ref[1:2, cols]
+            clean_key = clean_ref[1, :, cols].astype(jnp.float32)
+            query = keep * clean_ref[0, :, cols].astype(jnp.float32) + share * noise_ref[0, :, cols].astype(jnp.float32)
+            key = keep * clean_key + share * noise_ref[1, :, cols].astype(jnp.float32)
+            out_ref[0] = (clean_key * inverse[:, 2:3] * gain_k).astype(jnp.bfloat16)
+            out_ref[1] = (query * inverse[:, 0:1] * gain_q).astype(jnp.bfloat16)
+            out_ref[2] = (key * inverse[:, 1:2] * gain_k).astype(jnp.bfloat16)
+            offset += count
+
+
+def attention_kernel(place_ref, keep_ref, *refs):
+    value_refs, key_refs, halo_ref = refs[:4], refs[4:8], refs[8]
+    back_refs, ctx_ref, halo_grad_ref = refs[9:13], refs[13], refs[14]
+    keys, values, queries, own_keys, own_values, grads, back, key_acc, value_acc = refs[15:]
+    place, first = place_ref[0], place_ref[1]
+    scale = HEAD_DIM ** (-0.5)
+    for distance in range(GROUP):
+        spot = place ^ distance
+        keys[spot] = halo_ref[GROUP + distance]
+        values[spot] = halo_ref[distance]
+        keys[GROUP + spot] = key_refs[distance][0]
+        values[GROUP + spot] = value_refs[distance][0]
+        queries[spot] = key_refs[distance][1]
+        own_keys[spot] = key_refs[distance][2]
+        own_values[spot] = value_refs[distance][1]
+        grads[spot] = value_refs[distance][2]
+    key_acc[...] = jnp.zeros_like(key_acc)
+    value_acc[...] = jnp.zeros_like(value_acc)
+
+    def one_span(span, carry):
+        query, grad = queries[span], grads[span]
+        slots = [span + GROUP - hop for hop in range(1, CONTEXT + 1)]
+        key_blocks = [own_keys[span]] + [keys[slot] for slot in slots]
+        value_blocks = [own_values[span]] + [values[slot] for slot in slots]
+        absent = [0.0] + [
+            jnp.where(jnp.logical_and(first == 1, slot < GROUP), -masked_score, 0.0) for slot in slots
+        ]
+        scores = [contract(block, query, 1, 1) * (scale * LOG2E) for block in key_blocks]
+        top = functools.reduce(
+            jnp.maximum,
+            [jnp.max(part, axis=0, keepdims=True) - lack for part, lack in zip(scores, absent)],
+        )
+        exponents = [jnp.exp2(part - (top + lack)) for part, lack in zip(scores, absent)]
+        total = sum(jnp.sum(part, axis=0, keepdims=True) for part in exponents)
+        recip = 1.0 / total
+        attention = [part * recip for part in exponents]
+        weights = [part.astype(jnp.bfloat16) for part in attention]
+        output = sum(contract(block, part, 0, 0) for block, part in zip(value_blocks, weights))
+        grad_turned = jnp.transpose(grad.astype(jnp.float32))
+        delta = jnp.sum(output * grad_turned, axis=0, keepdims=True)
+        back[span, 0] = jnp.transpose(output).astype(jnp.bfloat16)
+        grad_query = 0.0
+        for index in range(CONTEXT + 1):
+            probs = contract(value_blocks[index], grad, 1, 1)
+            change = (attention[index] * (probs - delta) * scale).astype(jnp.bfloat16)
+            grad_query = grad_query + contract(key_blocks[index], change, 0, 0)
+            grad_key = jnp.dot(change, query, preferred_element_type=jnp.float32)
+            grad_value = jnp.dot(weights[index], grad, preferred_element_type=jnp.float32)
+            if index == 0:
+                back[span, 2] = grad_key.astype(jnp.bfloat16)
+                own_slot = GROUP + span
+                value_acc[own_slot] = value_acc[own_slot] + keep_ref[span ^ place] * grad_value
+            else:
+                slot = slots[index - 1]
+                key_acc[slot] = key_acc[slot] + grad_key
+                value_acc[slot] = value_acc[slot] + grad_value
+        back[span, 1] = jnp.transpose(grad_query).astype(jnp.bfloat16)
+        return carry
+
+    lax.fori_loop(0, GROUP, one_span, 0)
+    for distance in range(GROUP):
+        spot = place ^ distance
+        back_refs[distance][...] = back[spot]
+        ctx_ref[distance, 0] = key_acc[GROUP + spot]
+        ctx_ref[distance, 1] = value_acc[GROUP + spot]
+        halo_grad_ref[distance, 0] = key_acc[spot].astype(jnp.bfloat16)
+        halo_grad_ref[distance, 1] = value_acc[spot].astype(jnp.bfloat16)
+
+
+def noisy_at(clean_ref, noise_ref, index, cols, keep, share):
+    return keep * clean_ref[index, :, cols].astype(jnp.float32) + share * noise_ref[index, :, cols].astype(jnp.float32)
+
+
+def inner_kernel(width, sizes, place_ref, share_ref, clean_ref, noise_ref, gains_ref, *refs):
+    pieces = len(sizes) * GROUP
+    back_refs, ctx_refs = refs[:pieces], refs[pieces : 2 * pieces]
+    attended_ref, inner_ref = refs[2 * pieces :]
+    keep, share = share_ref[0], share_ref[1]
+    place = place_ref[0]
+    inner = [0.0, 0.0, 0.0]
+    for distance in range(GROUP):
+        offset = 0
+        for chunk, heads in enumerate(sizes):
+            count = heads * HEAD_DIM
+            cols = columns_at(place ^ distance, width, offset, count)
+            back_ref, ctx_ref = back_refs[chunk * GROUP + distance], ctx_refs[chunk * GROUP + distance]
+            gain_q, gain_k = gains_ref[0:1, cols], gains_ref[1:2, cols]
+            attended_ref[:, cols] = back_ref[0]
+            terms = (
+                noisy_at(clean_ref, noise_ref, 0, cols, keep, share) * gain_q * back_ref[1].astype(jnp.float32),
+                noisy_at(clean_ref, noise_ref, 1, cols, keep, share) * gain_k * back_ref[2].astype(jnp.float32),
+                clean_ref[1, :, cols].astype(jnp.float32) * gain_k * ctx_ref[0].astype(jnp.float32),
+            )
+            for index, term in enumerate(terms):
+                inner[index] = inner[index] + jnp.sum(term, axis=-1, keepdims=True)
+            offset += count
+    inner_ref[...] = pack_lanes(inner)
+
+
+def finish_kernel(
+    width, sizes, place_ref, share_ref, clean_ref, noise_ref, gains_ref,
+    sums_ref, sums_other_ref, inner_ref, inner_other_ref, *refs
+):
+    pieces = len(sizes) * GROUP
+    back_refs, ctx_refs, grads_ref = refs[:pieces], refs[pieces : 2 * pieces], refs[2 * pieces]
+    keep, share = share_ref[0], share_ref[1]
+    place = place_ref[0]
+    inverse = lax.rsqrt((sums_ref[...] + sums_other_ref[...]) / D + epsilon)
+    cube = inverse * inverse * inverse * ((inner_ref[...] + inner_other_ref[...]) / D)
+    for distance in range(GROUP):
+        offset = 0
+        for chunk, heads in enumerate(sizes):
+            count = heads * HEAD_DIM
+            cols = columns_at(place ^ distance, width, offset, count)
+            back_ref, ctx_ref = back_refs[chunk * GROUP + distance], ctx_refs[chunk * GROUP + distance]
+            gain_q, gain_k = gains_ref[0:1, cols], gains_ref[1:2, cols]
+            query = noisy_at(clean_ref, noise_ref, 0, cols, keep, share)
+            key = noisy_at(clean_ref, noise_ref, 1, cols, keep, share)
+            clean_key = clean_ref[1, :, cols].astype(jnp.float32)
+            grad_query = inverse[:, 0:1] * gain_q * back_ref[1].astype(jnp.float32) - query * cube[:, 0:1]
+            grad_own = inverse[:, 1:2] * gain_k * back_ref[2].astype(jnp.float32) - key * cube[:, 1:2]
+            grad_clean = inverse[:, 2:3] * gain_k * ctx_ref[0].astype(jnp.float32) - clean_key * cube[:, 2:3]
+            grads_ref[0, :, cols] = keep * grad_query
+            grads_ref[1, :, cols] = keep * grad_own + grad_clean
+            grads_ref[2, :, cols] = ctx_ref[1].astype(jnp.float32)
+            offset += count
+
+
+def on_group(clean_qkv, noise_qkv, timestep, gain_q, gain_k, attended_grad):
+    rows, local_width = clean_qkv.shape[1:]
+    width = local_width // GROUP
+    sizes = chunks_of(width // HEAD_DIM)
+    tm = lax.axis_index("tm")
+    group_count = lax.axis_size("tm") // GROUP
+    place = lax.rem(tm, GROUP)
+    first = (tm < GROUP).astype(jnp.int32)
+    places = jnp.stack([place, first]).astype(jnp.int32)
+    noise_share = noise_share_of(timestep[0])
+    keep_share = 1.0 - noise_share
+    shares = jnp.stack([keep_share, noise_share])
+    gains = jnp.stack([gain_q, gain_k])
+    keep_tile = jnp.full((8, 128), keep_share, jnp.float32)
+    keeps = jnp.stack([keep_share] + [swap(keep_tile, d)[0, 0] for d in range(1, GROUP)])
+
+    smem = pl.BlockSpec(memory_space=pltpu.SMEM)
+    params = pltpu.CompilerParams(vmem_limit_bytes=VMEM_LIMIT)
+    grid = (rows // ROWS,)
+
+    def by_rows(parts, count):
+        return pl.BlockSpec((parts, ROWS, count), lambda i: (0, i, 0))
+
+    flat = lambda count: pl.BlockSpec((ROWS, count), lambda i: (i, 0))
+    gain_spec = pl.BlockSpec((2, local_width), lambda i: (0, 0))
+
+    def bf16(*shape):
+        return jax.ShapeDtypeStruct(shape, jnp.bfloat16)
+
+    sums, *values = pl.pallas_call(
+        functools.partial(values_kernel, width),
+        grid=grid,
+        in_specs=[smem, smem, by_rows(3, local_width), by_rows(3, local_width), flat(local_width)],
+        out_specs=[flat(128)] + [by_rows(3, width)] * GROUP,
+        out_shape=[jax.ShapeDtypeStruct((rows, 128), jnp.float32)] + [bf16(3, rows, width)] * GROUP,
+        compiler_params=params,
+        cost_estimate=pl.CostEstimate(flops=30 * rows * local_width, bytes_accessed=22 * rows * local_width, transcendentals=0),
+        name="values",
+    )(places, shares, clean_qkv, noise_qkv, attended_grad)
+    sums_other = other_core(sums)
+    values = [values[0]] + [swap(values[d], d) for d in range(1, GROUP)]
+
+    keys = pl.pallas_call(
+        functools.partial(keys_kernel, width, sizes),
+        grid=grid,
+        in_specs=[smem, smem, by_rows(2, local_width), by_rows(2, local_width), gain_spec, flat(128), flat(128)],
+        out_specs=[by_rows(3, heads * HEAD_DIM) for heads in sizes for _ in range(GROUP)],
+        out_shape=[bf16(3, rows, heads * HEAD_DIM) for heads in sizes for _ in range(GROUP)],
+        compiler_params=params,
+        cost_estimate=pl.CostEstimate(flops=30 * rows * local_width, bytes_accessed=14 * rows * local_width, transcendentals=0),
+        name="keys",
+    )(places, shares, clean_qkv, noise_qkv, gains, sums, sums_other)
+
+    total = lax.axis_size("tm")
+    up = [(i, i + GROUP) for i in range(total - GROUP)]
+    down = [(i + GROUP, i) for i in range(total - GROUP)]
+    backs, ctxs = [], []
+    offset = 0
+    for chunk, heads in enumerate(sizes):
+        count = heads * HEAD_DIM
+        mine = keys[chunk * GROUP : (chunk + 1) * GROUP]
+        key_parts = [mine[0]] + [swap(mine[d], d) for d in range(1, GROUP)]
+        halo = jnp.stack(
+            [part[0, :, offset : offset + count] for part in values] + [part[0] for part in key_parts]
+        )
+        halo = lax.ppermute(halo, "tm", up)
+        at = offset // HEAD_DIM
+        one = lambda lead, start=0: pl.BlockSpec(lead + (rows, HEAD_DIM), lambda h: (0,) * len(lead) + (0, h + start))
+        *back, ctx, halo_grad = pl.pallas_call(
+            attention_kernel,
+            grid=(heads,),
+            in_specs=[smem, smem] + [one((3,), at)] * GROUP + [one((3,))] * GROUP + [one((2 * GROUP,))],
+            out_specs=[one((3,))] * GROUP + [one((GROUP, 2))] * 2,
+            out_shape=[bf16(3, rows, count)] * GROUP
+            + [jax.ShapeDtypeStruct((GROUP, 2, rows, count), jnp.float32), bf16(GROUP, 2, rows, count)],
+            scratch_shapes=[
+                pltpu.VMEM((2 * GROUP, rows, HEAD_DIM), jnp.bfloat16),
+                pltpu.VMEM((2 * GROUP, rows, HEAD_DIM), jnp.bfloat16),
+                pltpu.VMEM((GROUP, rows, HEAD_DIM), jnp.bfloat16),
+                pltpu.VMEM((GROUP, rows, HEAD_DIM), jnp.bfloat16),
+                pltpu.VMEM((GROUP, rows, HEAD_DIM), jnp.bfloat16),
+                pltpu.VMEM((GROUP, rows, HEAD_DIM), jnp.bfloat16),
+                pltpu.VMEM((GROUP, 3, rows, HEAD_DIM), jnp.bfloat16),
+                pltpu.VMEM((2 * GROUP, rows, HEAD_DIM), jnp.float32),
+                pltpu.VMEM((2 * GROUP, rows, HEAD_DIM), jnp.float32),
+            ],
+            compiler_params=params,
+            cost_estimate=pl.CostEstimate(
+                flops=heads * 2 * 12 * GROUP * (CONTEXT + 1) * rows * rows * HEAD_DIM,
+                bytes_accessed=heads * 64 * rows * HEAD_DIM * 2,
+                transcendentals=heads * GROUP * (CONTEXT + 1) * rows * rows,
+            ),
+            name="attention",
+        )(places, keeps, *values, *key_parts, halo)
+        backs += [back[0]] + [swap(back[d], d) for d in range(1, GROUP)]
+        later = lax.ppermute(halo_grad, "tm", down)
+        summed = [(ctx[d] + later[d].astype(jnp.float32)).astype(jnp.bfloat16) for d in range(GROUP)]
+        ctxs += [summed[0]] + [swap(summed[d], d) for d in range(1, GROUP)]
+        offset += count
+
+    piece_specs = [by_rows(3, heads * HEAD_DIM) for heads in sizes for _ in range(GROUP)]
+    ctx_specs = [by_rows(2, heads * HEAD_DIM) for heads in sizes for _ in range(GROUP)]
+    attended, inner = pl.pallas_call(
+        functools.partial(inner_kernel, width, sizes),
+        grid=grid,
+        in_specs=[smem, smem, by_rows(2, local_width), by_rows(2, local_width), gain_spec] + piece_specs + ctx_specs,
+        out_specs=[flat(local_width), flat(128)],
+        out_shape=[bf16(rows, local_width), jax.ShapeDtypeStruct((rows, 128), jnp.float32)],
+        compiler_params=params,
+        name="inner",
+    )(places, shares, clean_qkv, noise_qkv, gains, *backs, *ctxs)
+    inner_other = other_core(inner)
+    clean_grads = pl.pallas_call(
+        functools.partial(finish_kernel, width, sizes),
+        grid=grid,
+        in_specs=[smem, smem, by_rows(2, local_width), by_rows(2, local_width), gain_spec]
+        + [flat(128)] * 4 + piece_specs + ctx_specs,
+        out_specs=by_rows(3, local_width),
+        out_shape=jax.ShapeDtypeStruct((3, rows, local_width), jnp.float32),
+        compiler_params=params,
+        name="finish",
+    )(places, shares, clean_qkv, noise_qkv, gains, sums, sums_other, inner, inner_other, *backs, *ctxs)
+    return (attended, clean_grads)
+
+
 def solution(mesh):
     placed = (
         P(None, "tm", "head"),
@@ -157,8 +488,10 @@
         P("head"),
         P("tm", "head"),
     )
+    heads_here = D // HEAD_DIM // mesh.shape["head"]
+    grouped = mesh.shape["head"] == 2 and mesh.shape["tm"] % GROUP == 0 and heads_here % GROUP == 0
     return jax.shard_map(
-        on_device,
+        on_group if grouped else on_device,
         mesh=mesh,
         in_specs=placed,
         out_specs=(P("tm", "head"), P(None, "tm", "head")),

time: 1680 us -> 504 us (0.30)
  waiting for transfers between devices: 1090 us -> 255 us
  matrix products: 307 us -> 0 us
  other arithmetic: 186 us -> 5.18 us
  Pallas kernels: 0 us -> 154 us
  starting transfers between devices: 16.3 us -> 70.4 us
  local copies, waits for them, and re-layouts: 59.8 us -> 15.3 us
    ppermute x6 -> x41, waiting for transfers between devices: 1090 us -> 255 us  [the longest x33 254 us: swap(): lax.ppermute(block, 'tm', [(i, i ^ distance) for i in range(lax.axis_size...]
    dot_general x120 -> x0, matrix products: 307 us -> none  [the longest x80 212 us: contract(): lax.dot_general(left, right, (((left_dim,), (right_dim,)), ((), ())), pre...]
    pallas_call x0 -> x7, Pallas kernels: none -> 154 us  [the longest x3 103 us: on_group(): pl.pallas_call(attention_kernel, grid=(heads,), in_specs=[smem, smem] + [...]
    another operation x8 -> x4, other arithmetic: 59.7 us -> 2.14 us  [the longest x1 1.96 us: on_group(): jnp.stack([keep_share] + [swap(keep_tile, d)[0, 0] for d in range(1, GROU...]
    ppermute x6 -> x41, starting transfers between devices: 16.3 us -> 70.4 us  [the longest x33 42.6 us: swap(): lax.ppermute(block, 'tm', [(i, i ^ distance) for i in range(lax.axis_size...]
    convert_element_type x23 -> x3, other arithmetic: 53.3 us -> 3.04 us  [on_group(): (ctx[d] + later[d].astype(jnp.float32)).astype(jnp.bfloat16)]
    another operation x5, local copies, waits for them, and re-layouts: 46.1 us -> 0.83 us  [the longest x3 0.81 us: on_group(): jnp.stack([part[0, :, offset:offset + count] for part in values] + [part[...]
    reduce_sum x23 -> x0, other arithmetic: 33.8 us -> none  [the longest x20 18.9 us: one_head(): row_total = jnp.sum(exponent, axis=-1, keepdims=True)]
  transfers between devices with their start and end apart: 6 -> 41, of which waited for: 5 -> 22; matrix products, arithmetic and copies ran while one was open for 2% -> 3% of each run, Pallas kernels for 0% -> 23%
where the time goes in v1:
time: 504 us; the launch traced here: 501 us
  waiting for transfers between devices  255 us (51%)
  Pallas kernels  154 us (31%)
  starting transfers between devices  70.4 us (14%)
  local copies, waits for them, and re-layouts  15.3 us (3%)
  other arithmetic  5.18 us (1%)
    ppermute x33, waiting for transfers between devices, swap(): lax.ppermute(block, 'tm', [(i, i ^ distance) for i in range(lax.axis_size...  254 us
    pallas_call x3, Pallas kernels, on_group(): pl.pallas_call(attention_kernel, grid=(heads,), in_specs=[smem, smem] + [...  103 us
    ppermute x33, starting transfers between devices, swap(): lax.ppermute(block, 'tm', [(i, i ^ distance) for i in range(lax.axis_size...  42.6 us
    pallas_call x1, Pallas kernels, on_group(): pl.pallas_call(functools.partial(finish_kernel, width, sizes), grid=grid,...  16.7 us
    unnamed x105, local copies, waits for them, and re-layouts  12.9 us
    ppermute x3, starting transfers between devices, on_group(): halo = lax.ppermute(halo, 'tm', up)  12.4 us
    pallas_call x1, Pallas kernels, on_group(): pl.pallas_call(functools.partial(values_kernel, width), grid=grid, in_spe...  12.4 us
    pallas_call x1, Pallas kernels, on_group(): pl.pallas_call(functools.partial(inner_kernel, width, sizes), grid=grid,...  11.2 us
  transfers between devices with their start and end apart: 41, of which 22 were waited for; matrix products, arithmetic and copies ran while one was open for 3% of the time, Pallas kernels for 23%

profile of v1, /device:TPU:5, one launch (start us, length us, event | category | flops | bytes accessed | tf_op | source)
XLA Modules:
  0.0 501.3 jit_solution(14315967573780249846)
XLA Ops:
  1.5 12.4 %values.1 = (f32[512,128]{1,0:T(8,128)S(1)}, bf16[3,512,640]{2,1,0:T(8,128)(2,1)}, bf16[3,512,640]{2,1,0:T(8,128)(2,1)}, bf16[3,512,640]{2,1,0:T(8,128)(2,1)}, bf16[3,512,640]{2,1,0:T(8,128)(2,1)}) custom-call(s32[2]{0:T(128)S(1)} %pad_add_fusion.place_ref, f32[2]{0:T(128)S(1)} %pad_maximum_fusion.1.share_ref, bf16[3,512,2560]{2,1,0:T(8,128)(2,1)} %clean_ref.7, ...), custom_call_target="tpu_custom_call" | custom-call | flops 39321600 | bytes 28835840 | tf_op jit(solution)/shard_map/values/pallas_call | solution.py:386
  19.8 80.2 %collective-permute-done = f32[8,128]{1,0:T(8,128)S(1)} collective-permute-done((f32[8,128]{1,0:T(8,128)S(1)}, f32[8,128]{1,0:T(8,128)S(1)}, u32[]{:S(2)}, u32[]{:S(2)}) %collective-permute-start) | collective-permute-done | bytes 4128 | tf_op jit(solution)/shard_map/ppermute | solution.py:169
  108.2 10.2 %keys.1 = (bf16[3,512,256]{2,1,0:T(8,128)(2,1)}, bf16[3,512,256]{2,1,0:T(8,128)(2,1)}, bf16[3,512,256]{2,1,0:T(8,128)(2,1)}, bf16[3,512,256]{2,1,0:T(8,128)(2,1)...) custom-call(s32[2]{0:T(128)S(1)} %pad_add_fusion.place_ref, ...), custom_call_target="tpu_custom_call" | custom-call | flops 39321600 | bytes 18350080 | tf_op jit(solution)/shard_map/keys/pallas_call | solution.py:399
  130.1 5.9 %collective-permute-start.7 = (bf16[3,512,256]{2,1,0:T(8,128)(2,1)S(1)}, bf16[3,512,256]{2,1,0:T(8,128)(2,1)S(1)}, u32[]{:S(2)}, u32[]{:S(2)}) collective-permute-start(bf16[3,512,256]{2,1,0:T(8,128)(2,1)S(1)} %copy-done.41), channel_id=1, source_target_pairs={{0,2},{2,0},{4,6},{6,4},{8,10},{10,8},{12,14},{14,12},{16,18},{18,... | collective-permute-start | bytes 2359304 | tf_op jit(solution)/shard_map/ppermute | solution.py:169
  136.0 18.1 %collective-permute-done.14.refs_5_ = bf16[3,512,256]{2,1,0:T(8,128)(2,1)S(1)} collective-permute-done((bf16[3,512,256]{2,1,0:T(8,128)(2,1)}, bf16[3,512,256]{2,1,0:T(8,128)(2,1)S(1)}, u32[]{:S(2)}, u32[]{:S(2)}) %collective-permute-start.14) | collective-permute-done | bytes 786464 | tf_op jit(solution)/shard_map/ppermute | solution.py:169
  159.2 13.1 %collective-permute-done.16.refs_7_ = bf16[3,512,256]{2,1,0:T(8,128)(2,1)S(1)} collective-permute-done((bf16[3,512,256]{2,1,0:T(8,128)(2,1)S(1)}, bf16[3,512,256]{2,1,0:T(8,128)(2,1)S(1)}, u32[]{:S(2)}, u32[]{:S(2)}) %collective-permute-start.16) | collective-permute-done | bytes 786464 | tf_op jit(solution)/shard_map/ppermute | solution.py:169
  178.7 9.2 %collective-permute-done.7.refs_5_ = bf16[3,512,256]{2,1,0:T(8,128)(2,1)S(1)} collective-permute-done((bf16[3,512,256]{2,1,0:T(8,128)(2,1)S(1)}, bf16[3,512,256]{2,1,0:T(8,128)(2,1)S(1)}, u32[]{:S(2)}, u32[]{:S(2)}) %collective-permute-start.7) | collective-permute-done | bytes 786464 | tf_op jit(solution)/shard_map/ppermute | solution.py:169
  190.5 15.6 %collective-permute-done.9.refs_7_ = bf16[3,512,256]{2,1,0:T(8,128)(2,1)S(1)} collective-permute-done((bf16[3,512,256]{2,1,0:T(8,128)(2,1)S(1)}, bf16[3,512,256]{2,1,0:T(8,128)(2,1)S(1)}, u32[]{:S(2)}, u32[]{:S(2)}) %collective-permute-start.9) | collective-permute-done | bytes 786464 | tf_op jit(solution)/shard_map/ppermute | solution.py:169
  212.3 21.9 %attention.5 = (bf16[3,512,128]{2,1,0:T(8,128)(2,1)S(1)}, bf16[3,512,128]{2,1,0:T(8,128)(2,1)S(1)}, bf16[3,512,128]{2,1,0:T(8,128)(2,1)S(1)}, bf16[3,512,128]{2,...) custom-call(s32[2]{0:T(128)S(1)} %pad_add_fusion.place_ref, ...), custom_call_target="tpu_custom_call" | custom-call | flops 12884901888 | bytes 8388608 | tf_op jit(solution)/shard_map/attention/pallas_call | solution.py:425
  235.7 40.6 %attention.4 = (bf16[3,512,256]{2,1,0:T(8,128)(2,1)S(1)}, bf16[3,512,256]{2,1,0:T(8,128)(2,1)S(1)}, bf16[3,512,256]{2,1,0:T(8,128)(2,1)}, bf16[3,512,256]{2,1,0:...) custom-call(s32[2]{0:T(128)S(1)} %pad_add_fusion.place_ref, ...), custom_call_target="tpu_custom_call" | custom-call | flops 25769803776 | bytes 16777216 | tf_op jit(solution)/shard_map/attention/pallas_call | solution.py:425
  278.7 40.6 %attention.3 = (bf16[3,512,256]{2,1,0:T(8,128)(2,1)S(1)}, bf16[3,512,256]{2,1,0:T(8,128)(2,1)S(1)}, bf16[3,512,256]{2,1,0:T(8,128)(2,1)}, bf16[3,512,256]{2,1,0:...) custom-call(s32[2]{0:T(128)S(1)} %pad_add_fusion.place_ref, ...), custom_call_target="tpu_custom_call" | custom-call | flops 25769803776 | bytes 16777216 | tf_op jit(solution)/shard_map/attention/pallas_call | solution.py:425
  330.3 7.2 %collective-permute-done.26.refs_10_ = bf16[3,512,128]{2,1,0:T(8,128)(2,1)S(1)} collective-permute-done((bf16[3,512,128]{2,1,0:T(8,128)(2,1)S(1)}, bf16[3,512,128]{2,1,0:T(8,128)(2,1)S(1)}, u32[]{:S(2)}, u32[]{:S(2)}) %collective-permute-start.26) | collective-permute-done | bytes 393248 | tf_op jit(solution)/shard_map/ppermute | solution.py:169
  344.7 14.5 %collective-permute-done.38.refs_22_ = bf16[2,512,128]{2,1,0:T(8,128)(2,1)S(1)} collective-permute-done((bf16[2,512,128]{2,1,0:T(8,128)(2,1)S(1)}, bf16[2,512,128]{2,1,0:T(8,128)(2,1)S(1)}, u32[]{:S(2)}, u32[]{:S(2)}) %collective-permute-start.38) | collective-permute-done | bytes 262176 | tf_op jit(solution)/shard_map/ppermute | solution.py:169
  362.1 6.6 %collective-permute-done.39.refs_23_ = bf16[2,512,128]{2,1,0:T(8,128)(2,1)S(1)} collective-permute-done((bf16[2,512,128]{2,1,0:T(8,128)(2,1)S(1)}, bf16[2,512,128]{2,1,0:T(8,128)(2,1)S(1)}, u32[]{:S(2)}, u32[]{:S(2)}) %collective-permute-start.39) | collective-permute-done | bytes 262176 | tf_op jit(solution)/shard_map/ppermute | solution.py:169
  375.8 7.6 %collective-permute-done.20.refs_7_ = bf16[3,512,256]{2,1,0:T(8,128)(2,1)S(1)} collective-permute-done((bf16[3,512,256]{2,1,0:T(8,128)(2,1)S(1)}, bf16[3,512,256]{2,1,0:T(8,128)(2,1)S(1)}, u32[]{:S(2)}, u32[]{:S(2)}) %collective-permute-start.20) | collective-permute-done | bytes 786464 | tf_op jit(solution)/shard_map/ppermute | solution.py:169
  383.4 12.2 %collective-permute-done.11.refs_1_ = bf16[3,512,256]{2,1,0:T(8,128)(2,1)S(1)} collective-permute-done((bf16[3,512,256]{2,1,0:T(8,128)(2,1)S(1)}, bf16[3,512,256]{2,1,0:T(8,128)(2,1)S(1)}, u32[]{:S(2)}, u32[]{:S(2)}) %collective-permute-start.11) | collective-permute-done | bytes 786464 | tf_op jit(solution)/shard_map/ppermute | solution.py:169
  398.0 15.1 %collective-permute-done.12.refs_2_ = bf16[3,512,256]{2,1,0:T(8,128)(2,1)S(1)} collective-permute-done((bf16[3,512,256]{2,1,0:T(8,128)(2,1)}, bf16[3,512,256]{2,1,0:T(8,128)(2,1)S(1)}, u32[]{:S(2)}, u32[]{:S(2)}) %collective-permute-start.12) | collective-permute-done | bytes 786464 | tf_op jit(solution)/shard_map/ppermute | solution.py:169
  415.0 8.7 %collective-permute-done.33.refs_17_ = bf16[2,512,256]{2,1,0:T(8,128)(2,1)S(1)} collective-permute-done((bf16[2,512,256]{2,1,0:T(8,128)(2,1)S(1)}, bf16[2,512,256]{2,1,0:T(8,128)(2,1)S(1)}, u32[]{:S(2)}, u32[]{:S(2)}) %collective-permute-start.33) | collective-permute-done | bytes 524320 | tf_op jit(solution)/shard_map/ppermute | solution.py:169
  426.2 13.3 %collective-permute-done.34.refs_18_ = bf16[2,512,256]{2,1,0:T(8,128)(2,1)S(1)} collective-permute-done((bf16[2,512,256]{2,1,0:T(8,128)(2,1)S(1)}, bf16[2,512,256]{2,1,0:T(8,128)(2,1)S(1)}, u32[]{:S(2)}, u32[]{:S(2)}) %collective-permute-start.34) | collective-permute-done | bytes 524320 | tf_op jit(solution)/shard_map/ppermute | solution.py:169
  439.5 6.7 %collective-permute-done.29.refs_13_ = bf16[2,512,256]{2,1,0:T(8,128)(2,1)S(1)} collective-permute-done((bf16[2,512,256]{2,1,0:T(8,128)(2,1)S(1)}, bf16[2,512,256]{2,1,0:T(8,128)(2,1)S(1)}, u32[]{:S(2)}, u32[]{:S(2)}) %collective-permute-start.29) | collective-permute-done | bytes 524320 | tf_op jit(solution)/shard_map/ppermute | solution.py:169
  446.2 15.7 %collective-permute-done.30.refs_14_ = bf16[2,512,256]{2,1,0:T(8,128)(2,1)S(1)} collective-permute-done((bf16[2,512,256]{2,1,0:T(8,128)(2,1)S(1)}, bf16[2,512,256]{2,1,0:T(8,128)(2,1)S(1)}, u32[]{:S(2)}, u32[]{:S(2)}) %collective-permute-start.30) | collective-permute-done | bytes 524320 | tf_op jit(solution)/shard_map/ppermute | solution.py:169
  462.9 11.2 %inner.1 = (bf16[512,2560]{1,0:T(8,128)(2,1)}, f32[512,128]{1,0:T(8,128)S(1)}) custom-call(s32[2]{0:T(128)S(1)} %pad_add_fusion.place_ref, f32[2]{0:T(128)S(1)} %pad_maximum_fusion.1.share_ref, bf16[3,512,2560]{2,1,0:T(8,128)(2,1)} %clean_ref.7, bf16[3,512,2560]{2,1,0:T(8,128)(2,1)} %noise_ref.7, f32[2,2560]{1,0:T(2,128)S(1)} %pad_maximum_fusion.gains_ref, ...), custom_call_target="tpu_custom_call" | custom-call | tf_op jit(solution)/shard_map/inner/pallas_call | solution.py:459
  474.1 9.2 %collective-permute-start.40 = (f32[512,128]{1,0:T(8,128)S(1)}, f32[512,128]{1,0:T(8,128)S(1)}, u32[]{:S(2)}, u32[]{:S(2)}) collective-permute-start(f32[512,128]{1,0:T(8,128)S(1)} %get-tuple-element.75.inner_ref), channel_id=1, source_target_pairs={{0,1},{1,0},{2,3},{3,2},{4,5},{5,4},{6,7},{7,6},{8,9},{9,8},{10,11... | collective-permute-start | bytes 786440 | tf_op jit(solution)/shard_map/ppermute | solution.py:173
  484.4 16.7 %finish.1 = f32[3,512,2560]{2,1,0:T(8,128)} custom-call(s32[2]{0:T(128)S(1)} %pad_add_fusion.place_ref, f32[2]{0:T(128)S(1)} %pad_maximum_fusion.1.share_ref, bf16[3,512,2560]{2,1,0:T(8,128)(2,1)} %clean_ref.7, bf16[3,512,2560]{2,1,0:T(8,128)(2,1)} %noise_ref.7, f32[2,2560]{1,0:T(2,128)S(1)} %pad_maximum_fusion.gains_ref, ...), custom_call_target="tpu_custom_call" | custom-call | tf_op jit(solution)/shard_map/finish/pallas_call | solution.py:469
  (186 shorter events, 86.8 us)
Async XLA Ops:
  13.9 106.1 %collective-permute-start.3 = (bf16[3,512,640]{2,1,0:T(8,128)(2,1)}, bf16[3,512,640]{2,1,0:T(8,128)(2,1)S(1)}, u32[]{:S(2)}, u32[]{:S(2)}) collective-permute-start(bf16[3,512,640]{2,1,0:T(8,128)(2,1)} %get-tuple-element.40), channel_id=1, source_target_pairs={{0,2},{2,0},{4,6},{6,4},{8,10},{10,8},{12,14},{14,12},{16,18},{18,... | collective-permute-start | bytes 5898248 | tf_op jit(solution)/shard_map/ppermute | solution.py:169
  15.1 106.8 %collective-permute-start.4 = (bf16[3,512,640]{2,1,0:T(8,128)(2,1)}, bf16[3,512,640]{2,1,0:T(8,128)(2,1)S(1)}, u32[]{:S(2)}, u32[]{:S(2)}) collective-permute-start(bf16[3,512,640]{2,1,0:T(8,128)(2,1)} %get-tuple-element.41), channel_id=1, source_target_pairs={{0,4},{2,6},{4,0},{6,2},{8,12},{10,14},{12,8},{14,10},{16,20},{18,... | collective-permute-start | bytes 5898248 | tf_op jit(solution)/shard_map/ppermute | solution.py:169
  15.3 107.5 %collective-permute-start.5 = (bf16[3,512,640]{2,1,0:T(8,128)(2,1)}, bf16[3,512,640]{2,1,0:T(8,128)(2,1)S(1)}, u32[]{:S(2)}, u32[]{:S(2)}) collective-permute-start(bf16[3,512,640]{2,1,0:T(8,128)(2,1)} %get-tuple-element.42), channel_id=1, source_target_pairs={{0,6},{2,4},{4,2},{6,0},{8,14},{10,12},{12,10},{14,8},{16,22},{18,... | collective-permute-start | bytes 5898248 | tf_op jit(solution)/shard_map/ppermute | solution.py:169
  16.5 83.5 %collective-permute-start = (f32[8,128]{1,0:T(8,128)S(1)}, f32[8,128]{1,0:T(8,128)S(1)}, u32[]{:S(2)}, u32[]{:S(2)}) collective-permute-start(f32[8,128]{1,0:T(8,128)S(1)} %broadcast_in_dim.3), channel_id=1, source_target_pairs={{0,2},{2,0},{4,6},{6,4},{8,10},{10,8},{12,14},{14,12},{16,18},{18,... | collective-permute-start | bytes 12296 | tf_op jit(solution)/shard_map/ppermute | solution.py:169
  17.7 83.4 %collective-permute-start.1 = (f32[8,128]{1,0:T(8,128)S(1)}, f32[8,128]{1,0:T(8,128)S(1)}, u32[]{:S(2)}, u32[]{:S(2)}) collective-permute-start(f32[8,128]{1,0:T(8,128)S(1)} %broadcast_in_dim.3), channel_id=1, source_target_pairs={{0,4},{2,6},{4,0},{6,2},{8,12},{10,14},{12,8},{14,10},{16,20},{18,... | collective-permute-start | bytes 12296 | tf_op jit(solution)/shard_map/ppermute | solution.py:169
  119.9 35.8 %collective-permute-start.23 = (bf16[3,512,128]{2,1,0:T(8,128)(2,1)}, bf16[3,512,128]{2,1,0:T(8,128)(2,1)S(1)}, u32[]{:S(2)}, u32[]{:S(2)}) collective-permute-start(bf16[3,512,128]{2,1,0:T(8,128)(2,1)} %get-tuple-element.63), channel_id=1, source_target_pairs={{0,6},{2,4},{4,2},{6,0},{8,14},{10,12},{12,10},{14,8},{16,22},{18,... | collective-permute-start | bytes 1179656 | tf_op jit(solution)/shard_map/ppermute | solution.py:169
  128.7 43.6 %collective-permute-start.16 = (bf16[3,512,256]{2,1,0:T(8,128)(2,1)S(1)}, bf16[3,512,256]{2,1,0:T(8,128)(2,1)S(1)}, u32[]{:S(2)}, u32[]{:S(2)}) collective-permute-start(bf16[3,512,256]{2,1,0:T(8,128)(2,1)S(1)} %copy-done.42), channel_id=1, source_target_pairs={{0,6},{2,4},{4,2},{6,0},{8,14},{10,12},{12,10},{14,8},{16,22},{18,... | collective-permute-start | bytes 2359304 | tf_op jit(solution)/shard_map/ppermute | solution.py:169
  130.1 57.7 %collective-permute-start.7 = (bf16[3,512,256]{2,1,0:T(8,128)(2,1)S(1)}, bf16[3,512,256]{2,1,0:T(8,128)(2,1)S(1)}, u32[]{:S(2)}, u32[]{:S(2)}) collective-permute-start(bf16[3,512,256]{2,1,0:T(8,128)(2,1)S(1)} %copy-done.41), channel_id=1, source_target_pairs={{0,2},{2,0},{4,6},{6,4},{8,10},{10,8},{12,14},{14,12},{16,18},{18,... | collective-permute-start | bytes 2359304 | tf_op jit(solution)/shard_map/ppermute | solution.py:169
  154.1 35.6 %collective-permute-start.8 = (bf16[3,512,256]{2,1,0:T(8,128)(2,1)S(1)}, bf16[3,512,256]{2,1,0:T(8,128)(2,1)S(1)}, u32[]{:S(2)}, u32[]{:S(2)}) collective-permute-start(bf16[3,512,256]{2,1,0:T(8,128)(2,1)S(1)} %copy-done.40), channel_id=1, source_target_pairs={{0,4},{2,6},{4,0},{6,2},{8,12},{10,14},{12,8},{14,10},{16,20},{18,... | collective-permute-start | bytes 2359304 | tf_op jit(solution)/shard_map/ppermute | solution.py:169
  155.8 50.3 %collective-permute-start.9 = (bf16[3,512,256]{2,1,0:T(8,128)(2,1)S(1)}, bf16[3,512,256]{2,1,0:T(8,128)(2,1)S(1)}, u32[]{:S(2)}, u32[]{:S(2)}) collective-permute-start(bf16[3,512,256]{2,1,0:T(8,128)(2,1)S(1)} %copy-done.39), channel_id=1, source_target_pairs={{0,6},{2,4},{4,2},{6,0},{8,14},{10,12},{12,10},{14,8},{16,22},{18,... | collective-permute-start | bytes 2359304 | tf_op jit(solution)/shard_map/ppermute | solution.py:169
  155.9 55.4 %collective-permute-start.24 = (bf16[8,512,128]{2,1,0:T(8,128)(2,1)S(1)}, bf16[8,512,128]{2,1,0:T(8,128)(2,1)S(1)}, u32[]{:S(2)}, u32[]{:S(2)}) collective-permute-start(bf16[8,512,128]{2,1,0:T(8,128)(2,1)S(1)} %slice_dynamic-update-slice_fusion.16), channel_id=1, source_target_pairs={{0,8},{2,10},{4,12},{6,14},{8,16},{10,18},{12,20},{14,22},{16,24},... | collective-permute-start | bytes 3145736 | tf_op jit(solution)/shard_map/ppermute | solution.py:422
  172.4 63.4 %collective-permute-start.17 = (bf16[8,512,256]{2,1,0:T(8,128)(2,1)S(1)}, bf16[8,512,256]{2,1,0:T(8,128)(2,1)}, u32[]{:S(2)}, u32[]{:S(2)}) collective-permute-start(bf16[8,512,256]{2,1,0:T(8,128)(2,1)S(1)} %slice_dynamic-update-slice_fusion), channel_id=1, source_target_pairs={{0,8},{2,10},{4,12},{6,14},{8,16},{10,18},{12,20},{14,22},{16,24},... | collective-permute-start | bytes 6291464 | tf_op jit(solution)/shard_map/ppermute | solution.py:422
  206.8 71.8 %collective-permute-start.10 = (bf16[8,512,256]{2,1,0:T(8,128)(2,1)}, bf16[8,512,256]{2,1,0:T(8,128)(2,1)}, u32[]{:S(2)}, u32[]{:S(2)}) collective-permute-start(bf16[8,512,256]{2,1,0:T(8,128)(2,1)} %slice_dynamic-update-slice_fusion.6), channel_id=1, source_target_pairs={{0,8},{2,10},{4,12},{6,14},{8,16},{10,18},{12,20},{14,22},{16,24},... | collective-permute-start | bytes 6291464 | tf_op jit(solution)/shard_map/ppermute | solution.py:422
  234.3 92.7 %collective-permute-start.36 = (bf16[4,2,512,128]{3,2,1,0:T(8,128)(2,1)}, bf16[4,2,512,128]{3,2,1,0:T(8,128)(2,1)S(1)}, u32[]{:S(2)}, u32[]{:S(2)}) collective-permute-start(bf16[4,2,512,128]{3,2,1,0:T(8,128)(2,1)} %get-tuple-element.73), channel_id=1, source_target_pairs={{8,0},{10,2},{12,4},{14,6},{16,8},{18,10},{20,12},{22,14},{24,16},... | collective-permute-start | bytes 3145736 | tf_op jit(solution)/shard_map/ppermute | solution.py:452
  277.3 94.1 %collective-permute-start.32 = (bf16[4,2,512,256]{3,2,1,0:T(8,128)(2,1)}, bf16[4,2,512,256]{3,2,1,0:T(8,128)(2,1)S(1)}, u32[]{:S(2)}, u32[]{:S(2)}) collective-permute-start(bf16[4,2,512,256]{3,2,1,0:T(8,128)(2,1)} %get-tuple-element.71), channel_id=1, source_target_pairs={{8,0},{10,2},{12,4},{14,6},{16,8},{18,10},{20,12},{22,14},{24,16},... | collective-permute-start | bytes 6291464 | tf_op jit(solution)/shard_map/ppermute | solution.py:452
  319.4 54.1 %collective-permute-start.28 = (bf16[4,2,512,256]{3,2,1,0:T(8,128)(2,1)}, bf16[4,2,512,256]{3,2,1,0:T(8,128)(2,1)S(1)}, u32[]{:S(2)}, u32[]{:S(2)}) collective-permute-start(bf16[4,2,512,256]{3,2,1,0:T(8,128)(2,1)} %get-tuple-element.69), channel_id=1, source_target_pairs={{8,0},{10,2},{12,4},{14,6},{16,8},{18,10},{20,12},{22,14},{24,16},... | collective-permute-start | bytes 6291464 | tf_op jit(solution)/shard_map/ppermute | solution.py:452
  369.5 43.6 %collective-permute-start.12 = (bf16[3,512,256]{2,1,0:T(8,128)(2,1)}, bf16[3,512,256]{2,1,0:T(8,128)(2,1)S(1)}, u32[]{:S(2)}, u32[]{:S(2)}) collective-permute-start(bf16[3,512,256]{2,1,0:T(8,128)(2,1)} %get-tuple-element.50), channel_id=1, source_target_pairs={{0,4},{2,6},{4,0},{6,2},{8,12},{10,14},{12,8},{14,10},{16,20},{18,... | collective-permute-start | bytes 2359304 | tf_op jit(solution)/shard_map/ppermute | solution.py:169
  371.4 43.6 %collective-permute-start.13 = (bf16[3,512,256]{2,1,0:T(8,128)(2,1)}, bf16[3,512,256]{2,1,0:T(8,128)(2,1)S(1)}, u32[]{:S(2)}, u32[]{:S(2)}) collective-permute-start(bf16[3,512,256]{2,1,0:T(8,128)(2,1)} %get-tuple-element.51), channel_id=1, source_target_pairs={{0,6},{2,4},{4,2},{6,0},{8,14},{10,12},{12,10},{14,8},{16,22},{18,... | collective-permute-start | bytes 2359304 | tf_op jit(solution)/shard_map/ppermute | solution.py:169
  373.4 50.3 %collective-permute-start.33 = (bf16[2,512,256]{2,1,0:T(8,128)(2,1)S(1)}, bf16[2,512,256]{2,1,0:T(8,128)(2,1)S(1)}, u32[]{:S(2)}, u32[]{:S(2)}) collective-permute-start(bf16[2,512,256]{2,1,0:T(8,128)(2,1)S(1)} %get-tuple-element.78), channel_id=1, source_target_pairs={{0,2},{2,0},{4,6},{6,4},{8,10},{10,8},{12,14},{14,12},{16,18},{18,... | collective-permute-start | bytes 1572872 | tf_op jit(solution)/shard_map/ppermute | solution.py:169
  383.4 56.1 %collective-permute-start.34 = (bf16[2,512,256]{2,1,0:T(8,128)(2,1)S(1)}, bf16[2,512,256]{2,1,0:T(8,128)(2,1)S(1)}, u32[]{:S(2)}, u32[]{:S(2)}) collective-permute-start(bf16[2,512,256]{2,1,0:T(8,128)(2,1)S(1)} %get-tuple-element.77), channel_id=1, source_target_pairs={{0,4},{2,6},{4,0},{6,2},{8,12},{10,14},{12,8},{14,10},{16,20},{18,... | collective-permute-start | bytes 1572872 | tf_op jit(solution)/shard_map/ppermute | solution.py:169
  395.6 43.9 %collective-permute-start.35 = (bf16[2,512,256]{2,1,0:T(8,128)(2,1)S(1)}, bf16[2,512,256]{2,1,0:T(8,128)(2,1)S(1)}, u32[]{:S(2)}, u32[]{:S(2)}) collective-permute-start(bf16[2,512,256]{2,1,0:T(8,128)(2,1)S(1)} %get-tuple-element.76), channel_id=1, source_target_pairs={{0,6},{2,4},{4,2},{6,0},{8,14},{10,12},{12,10},{14,8},{16,22},{18,... | collective-permute-start | bytes 1572872 | tf_op jit(solution)/shard_map/ppermute | solution.py:169
  413.1 33.1 %collective-permute-start.29 = (bf16[2,512,256]{2,1,0:T(8,128)(2,1)S(1)}, bf16[2,512,256]{2,1,0:T(8,128)(2,1)S(1)}, u32[]{:S(2)}, u32[]{:S(2)}) collective-permute-start(bf16[2,512,256]{2,1,0:T(8,128)(2,1)S(1)} %get-tuple-element.82), channel_id=1, source_target_pairs={{0,2},{2,0},{4,6},{6,4},{8,10},{10,8},{12,14},{14,12},{16,18},{18,... | collective-permute-start | bytes 1572872 | tf_op jit(solution)/shard_map/ppermute | solution.py:169
  415.0 46.9 %collective-permute-start.30 = (bf16[2,512,256]{2,1,0:T(8,128)(2,1)S(1)}, bf16[2,512,256]{2,1,0:T(8,128)(2,1)S(1)}, u32[]{:S(2)}, u32[]{:S(2)}) collective-permute-start(bf16[2,512,256]{2,1,0:T(8,128)(2,1)S(1)} %get-tuple-element.81), channel_id=1, source_target_pairs={{0,4},{2,6},{4,0},{6,2},{8,12},{10,14},{12,8},{14,10},{16,20},{18,... | collective-permute-start | bytes 1572872 | tf_op jit(solution)/shard_map/ppermute | solution.py:169
  423.7 38.2 %collective-permute-start.31 = (bf16[2,512,256]{2,1,0:T(8,128)(2,1)S(1)}, bf16[2,512,256]{2,1,0:T(8,128)(2,1)S(1)}, u32[]{:S(2)}, u32[]{:S(2)}) collective-permute-start(bf16[2,512,256]{2,1,0:T(8,128)(2,1)S(1)} %get-tuple-element.80), channel_id=1, source_target_pairs={{0,6},{2,4},{4,2},{6,0},{8,14},{10,12},{12,10},{14,8},{16,22},{18,... | collective-permute-start | bytes 1572872 | tf_op jit(solution)/shard_map/ppermute | solution.py:169
  (61 other events, 1987.4 us)

commit v2 on v0

--- a/solution.py
+++ b/solution.py
@@ -1,6 +1,9 @@
+import functools
 import jax
 import jax.numpy as jnp
 from jax import lax
+from jax.experimental import pallas as pl
+from jax.experimental.pallas import tpu as pltpu
 from jax.sharding import PartitionSpec as P
 
 D = 5120
@@ -148,6 +151,472 @@
     return (attended, clean_grads)
 
 
+GROUP = 4
+ROWS = 64
+LOG2E = 1.4426950408889634
+VMEM_LIMIT = 48 * 1024 * 1024
+EXCHANGE_VMEM = 62 * 1024 * 1024
+
+
+def other_core(block):
+    return lax.ppermute(block, "head", [(0, 1), (1, 0)])
+
+
+def columns_at(place, width, offset, count):
+    return pl.ds(pl.multiple_of(place * width + offset, HEAD_DIM), count)
+
+
+def pack_lanes(parts):
+    lane = lax.broadcasted_iota(jnp.int32, (parts[0].shape[0], 128), 1)
+    packed = jnp.zeros((parts[0].shape[0], 128), jnp.float32)
+    for index, part in enumerate(parts):
+        packed = jnp.where(lane == index, part, packed)
+    return packed
+
+
+def sums_kernel(share_ref, clean_ref, noise_ref, sums_ref):
+    keep, share = share_ref[0], share_ref[1]
+    clean_key = clean_ref[1].astype(jnp.float32)
+    query = keep * clean_ref[0].astype(jnp.float32) + share * noise_ref[0].astype(jnp.float32)
+    key = keep * clean_key + share * noise_ref[1].astype(jnp.float32)
+    sums_ref[...] = pack_lanes([jnp.sum(field * field, axis=-1, keepdims=True) for field in (query, key, clean_key)])
+
+
+def pack_kernel(heads, place_ref, share_ref, clean_ref, noise_ref, grad_ref, gains_ref, sums_ref, other_ref, packed_ref):
+    keep, share = share_ref[0], share_ref[1]
+    place = place_ref[0]
+    inverse = lax.rsqrt((sums_ref[...] + other_ref[...]) / D + epsilon)
+    for distance in range(GROUP):
+        for head in range(heads):
+            cols = columns_at(place ^ distance, heads * HEAD_DIM, head * HEAD_DIM, HEAD_DIM)
+            gain_q, gain_k = gains_ref[0:1, cols], gains_ref[1:2, cols]
+            clean_value = clean_ref[2, :, cols]
+            clean_key = clean_ref[1, :, cols].astype(jnp.float32)
+            query = keep * clean_ref[0, :, cols].astype(jnp.float32) + share * noise_ref[0, :, cols].astype(jnp.float32)
+            key = keep * clean_key + share * noise_ref[1, :, cols].astype(jnp.float32)
+            value = keep * clean_value.astype(jnp.float32) + share * noise_ref[2, :, cols].astype(jnp.float32)
+            packed_ref[head, distance, 0] = clean_value
+            packed_ref[head, distance, 1] = (clean_key * inverse[:, 2:3] * gain_k).astype(jnp.bfloat16)
+            packed_ref[head, distance, 2] = value.astype(jnp.bfloat16)
+            packed_ref[head, distance, 3] = (key * inverse[:, 1:2] * gain_k).astype(jnp.bfloat16)
+            packed_ref[head, distance, 4] = (query * inverse[:, 0:1] * gain_q).astype(jnp.bfloat16)
+            packed_ref[head, distance, 5] = grad_ref[:, cols]
+
+
+BACK_SLOTS = 3
+
+
+def exchange_kernel(
+    heads, layers, packed_ref, keep_ref, home_ref,
+    taken, halo, halo_back, back, halo_out, keeps, keys, values, key_acc, value_acc,
+    own_sem, take_send, take_recv, keep_send, keep_recv, up_send, up_recv, down_send, down_recv,
+    own_back_sem, back_send, back_recv, own_ctx_sem, ctx_send, ctx_recv,
+):
+    tm = lax.axis_index("tm")
+    total = layers * GROUP
+    layer, place = lax.div(tm, GROUP), lax.rem(tm, GROUP)
+    low, high = lax.rem(place, 2), lax.div(place, 2)
+    not_first = lax.div(layer + layers - 1, layers)
+    not_last = lax.div(2 * layers - 2 - layer, layers)
+    scale = HEAD_DIM ** (-0.5)
+
+    def across(spot):
+        return lax.rem(lax.rem(spot, 2) + low, 2) + 2 * lax.rem(lax.div(spot, 2) + high, 2)
+
+    def partner(distance):
+        return {"tm": layer * GROUP + across(jnp.int32(distance))}
+
+    def remote(src, dst, send, recv, target):
+        return pltpu.make_async_remote_copy(
+            src_ref=src, dst_ref=dst, send_sem=send, recv_sem=recv,
+            device_id=target, device_id_type=pl.DeviceIdType.MESH,
+        )
+
+    def own(head):
+        return pltpu.make_async_copy(packed_ref.at[head, 0], taken.at[head, 0], own_sem.at[head])
+
+    def take(head, d):
+        return remote(
+            packed_ref.at[head, d], taken.at[head, d], take_send.at[head, d], take_recv.at[head, d], partner(d)
+        )
+
+    def keep_copy(d):
+        return remote(keep_ref, keeps.at[d], keep_send.at[d], keep_recv.at[d], partner(d))
+
+    def up(head):
+        return remote(
+            taken.at[head, :, pl.ds(0, 2)], halo.at[head], up_send.at[head], up_recv.at[head], {"tm": lax.rem(tm + GROUP, total)}
+        )
+
+    def down(head):
+        return remote(
+            halo_out.at[lax.rem(head, 2)], halo_back.at[head], down_send.at[head], down_recv.at[head], {"tm": lax.rem(tm + total - GROUP, total)}
+        )
+
+    def own_back(head):
+        return pltpu.make_async_copy(
+            back.at[lax.rem(head, BACK_SLOTS), 0, pl.ds(0, 3)], home_ref.at[head, 0, pl.ds(0, 3)], own_back_sem.at[head]
+        )
+
+    def give(head, d):
+        return remote(
+            back.at[lax.rem(head, BACK_SLOTS), d, pl.ds(0, 3)], home_ref.at[head, d, pl.ds(0, 3)],
+            back_send.at[head, d], back_recv.at[head, d], partner(d),
+        )
+
+    def own_ctx(head):
+        return pltpu.make_async_copy(
+            back.at[lax.rem(head, BACK_SLOTS), 0, pl.ds(3, 2)], home_ref.at[head, 0, pl.ds(3, 2)], own_ctx_sem.at[head]
+        )
+
+    def give_ctx(head, d):
+        return remote(
+            back.at[lax.rem(head, BACK_SLOTS), d, pl.ds(3, 2)], home_ref.at[head, d, pl.ds(3, 2)],
+            ctx_send.at[head, d], ctx_recv.at[head, d], partner(d),
+        )
+
+    def start_take(head):
+        own(head).start()
+        for d in range(1, GROUP):
+            take(head, d).start()
+
+    def drain_sends(head):
+        own_back(head).wait()
+        own_ctx(head).wait()
+        for d in range(1, GROUP):
+            give(head, d).wait_send()
+            give_ctx(head, d).wait_send()
+
+    barrier = pltpu.get_barrier_semaphore()
+    for d in range(1, GROUP):
+        pl.semaphore_signal(barrier, inc=1, device_id=partner(d), device_id_type=pl.DeviceIdType.MESH)
+
+    @pl.when(not_first == 1)
+    def _():
+        pl.semaphore_signal(barrier, inc=1, device_id={"tm": tm - GROUP}, device_id_type=pl.DeviceIdType.MESH)
+
+    @pl.when(not_last == 1)
+    def _():
+        pl.semaphore_signal(barrier, inc=1, device_id={"tm": tm + GROUP}, device_id_type=pl.DeviceIdType.MESH)
+
+    pl.semaphore_wait(barrier, GROUP - 1 + not_first + not_last)
+
+    for d in range(1, GROUP):
+        keep_copy(d).start()
+    for head in range(min(2, heads)):
+        start_take(jnp.int32(head))
+    keeps[0] = keep_ref[...]
+    for d in range(1, GROUP):
+        keep_copy(d).wait_recv()
+
+    def attention(head):
+        parity = lax.rem(head, 2)
+        slot_back = lax.rem(head, BACK_SLOTS)
+        for distance in range(GROUP):
+            spot = across(jnp.int32(distance))
+            values[spot] = halo[head, distance, 0]
+            keys[spot] = halo[head, distance, 1]
+            values[GROUP + spot] = taken[head, distance, 0]
+            keys[GROUP + spot] = taken[head, distance, 1]
+        key_acc[parity] = jnp.zeros(key_acc.shape[1:], jnp.float32)
+        value_acc[parity] = jnp.zeros(value_acc.shape[1:], jnp.float32)
+
+        def one_span(span, carry):
+            d = across(span)
+            query, grad = taken[head, d, 4], taken[head, d, 5]
+            slots = [span + GROUP - hop for hop in range(1, CONTEXT + 1)]
+            key_blocks = [taken[head, d, 3]] + [keys[slot] for slot in slots]
+            value_blocks = [taken[head, d, 2]] + [values[slot] for slot in slots]
+            absent = [0.0] + [
+                jnp.where(jnp.logical_and(not_first == 0, slot < GROUP), -masked_score, 0.0) for slot in slots
+            ]
+            scores = [contract(block, query, 1, 1) * (scale * LOG2E) for block in key_blocks]
+            top = functools.reduce(
+                jnp.maximum,
+                [jnp.max(part, axis=0, keepdims=True) - lack for part, lack in zip(scores, absent)],
+            )
+            exponents = [jnp.exp2(part - (top + lack)) for part, lack in zip(scores, absent)]
+            total = sum(jnp.sum(part, axis=0, keepdims=True) for part in exponents)
+            recip = 1.0 / total
+            attention = [part * recip for part in exponents]
+            weights = [part.astype(jnp.bfloat16) for part in attention]
+            output = sum(contract(block, part, 0, 0) for block, part in zip(value_blocks, weights))
+            grad_turned = jnp.transpose(grad.astype(jnp.float32))
+            delta = jnp.sum(output * grad_turned, axis=0, keepdims=True)
+            back[slot_back, d, 0] = jnp.transpose(output).astype(jnp.bfloat16)
+            grad_query = 0.0
+            for index in range(CONTEXT + 1):
+                probs = contract(value_blocks[index], grad, 1, 1)
+                change = (attention[index] * (probs - delta) * scale).astype(jnp.bfloat16)
+                grad_query = grad_query + contract(key_blocks[index], change, 0, 0)
+                grad_key = jnp.dot(change, query, preferred_element_type=jnp.float32)
+                grad_value = jnp.dot(weights[index], grad, preferred_element_type=jnp.float32)
+                if index == 0:
+                    back[slot_back, d, 2] = grad_key.astype(jnp.bfloat16)
+                    own_slot = GROUP + span
+                    value_acc[parity, own_slot] = value_acc[parity, own_slot] + keeps[d, 0:1] * grad_value
+                else:
+                    slot = slots[index - 1]
+                    key_acc[parity, slot] = key_acc[parity, slot] + grad_key
+                    value_acc[parity, slot] = value_acc[parity, slot] + grad_value
+            back[slot_back, d, 1] = jnp.transpose(grad_query).astype(jnp.bfloat16)
+            return carry
+
+        lax.fori_loop(0, GROUP, one_span, 0)
+        for distance in range(GROUP):
+            spot = across(jnp.int32(distance))
+            halo_out[parity, distance, 0] = value_acc[parity, spot].astype(jnp.bfloat16)
+            halo_out[parity, distance, 1] = key_acc[parity, spot].astype(jnp.bfloat16)
+
+    def step(index, carry):
+        @pl.when(index < heads)
+        def _():
+            own(index).wait()
+            for d in range(1, GROUP):
+                take(index, d).wait_recv()
+
+            @pl.when(not_last == 1)
+            def _():
+                up(index).start()
+
+            @pl.when(index + 2 < heads)
+            def _():
+                start_take(index + 2)
+
+            @pl.when(not_first == 0)
+            def _():
+                halo[index] = jnp.zeros(halo.shape[1:], halo.dtype)
+
+        @pl.when(jnp.logical_and(index >= 1, index <= heads))
+        def _():
+            head = index - 1
+
+            @pl.when(not_first == 1)
+            def _():
+                up(head).wait_recv()
+
+            @pl.when(head >= BACK_SLOTS)
+            def _():
+                drain_sends(head - BACK_SLOTS)
+
+            @pl.when(jnp.logical_and(head >= 2, not_first == 1))
+            def _():
+                down(head - 2).wait_send()
+
+            attention(head)
+            own_back(head).start()
+            for d in range(1, GROUP):
+                give(head, d).start()
+
+            @pl.when(not_first == 1)
+            def _():
+                down(head).start()
+
+        @pl.when(index >= 2)
+        def _():
+            head = index - 2
+            parity = lax.rem(head, 2)
+            slot_back = lax.rem(head, BACK_SLOTS)
+
+            @pl.when(not_last == 1)
+            def _():
+                down(head).wait_recv()
+
+            @pl.when(not_last == 0)
+            def _():
+                halo_back[head] = jnp.zeros(halo_back.shape[1:], halo_back.dtype)
+
+            for distance in range(GROUP):
+                spot = GROUP + across(jnp.int32(distance))
+                grad_key = key_acc[parity, spot] + halo_back[head, distance, 1].astype(jnp.float32)
+                grad_value = value_acc[parity, spot] + halo_back[head, distance, 0].astype(jnp.float32)
+                back[slot_back, distance, 3] = grad_key.astype(jnp.bfloat16)
+                back[slot_back, distance, 4] = grad_value.astype(jnp.bfloat16)
+            own_ctx(head).start()
+            for d in range(1, GROUP):
+                give_ctx(head, d).start()
+
+        return carry
+
+    lax.fori_loop(0, heads + 2, step, 0)
+
+    def finish_head(head, carry):
+        for d in range(1, GROUP):
+            take(head, d).wait_send()
+            give(head, d).wait_recv()
+            give_ctx(head, d).wait_recv()
+
+        @pl.when(not_last == 1)
+        def _():
+            up(head).wait_send()
+
+        @pl.when(head >= heads - BACK_SLOTS)
+        def _():
+            drain_sends(head)
+
+        @pl.when(jnp.logical_and(head >= heads - 2, not_first == 1))
+        def _():
+            down(head).wait_send()
+
+        return carry
+
+    lax.fori_loop(0, heads, finish_head, 0)
+    for d in range(1, GROUP):
+        keep_copy(d).wait_send()
+
+
+def noisy_at(clean_ref, noise_ref, index, cols, keep, share):
+    return keep * clean_ref[index, :, cols].astype(jnp.float32) + share * noise_ref[index, :, cols].astype(jnp.float32)
+
+
+def inner_kernel(heads, place_ref, share_ref, clean_ref, noise_ref, gains_ref, home_ref, inner_ref):
+    keep, share = share_ref[0], share_ref[1]
+    place = place_ref[0]
+    inner = [0.0, 0.0, 0.0]
+    for distance in range(GROUP):
+        for head in range(heads):
+            cols = columns_at(place ^ distance, heads * HEAD_DIM, head * HEAD_DIM, HEAD_DIM)
+            gain_q, gain_k = gains_ref[0:1, cols], gains_ref[1:2, cols]
+            terms = (
+                noisy_at(clean_ref, noise_ref, 0, cols, keep, share) * gain_q * home_ref[head, distance, 1].astype(jnp.float32),
+                noisy_at(clean_ref, noise_ref, 1, cols, keep, share) * gain_k * home_ref[head, distance, 2].astype(jnp.float32),
+                clean_ref[1, :, cols].astype(jnp.float32) * gain_k * home_ref[head, distance, 3].astype(jnp.float32),
+            )
+            for index, term in enumerate(terms):
+                inner[index] = inner[index] + term
+    inner_ref[...] = pack_lanes([jnp.sum(part, axis=-1, keepdims=True) for part in inner])
+
+
+def finish_kernel(
+    heads, place_ref, share_ref, clean_ref, noise_ref, gains_ref,
+    sums_ref, sums_other_ref, inner_ref, inner_other_ref, home_ref, attended_ref, grads_ref
+):
+    keep, share = share_ref[0], share_ref[1]
+    place = place_ref[0]
+    inverse = lax.rsqrt((sums_ref[...] + sums_other_ref[...]) / D + epsilon)
+    cube = inverse * inverse * inverse * ((inner_ref[...] + inner_other_ref[...]) / D)
+    for distance in range(GROUP):
+        for head in range(heads):
+            cols = columns_at(place ^ distance, heads * HEAD_DIM, head * HEAD_DIM, HEAD_DIM)
+            gain_q, gain_k = gains_ref[0:1, cols], gains_ref[1:2, cols]
+            query = noisy_at(clean_ref, noise_ref, 0, cols, keep, share)
+            key = noisy_at(clean_ref, noise_ref, 1, cols, keep, share)
+            clean_key = clean_ref[1, :, cols].astype(jnp.float32)
+            grad = [home_ref[head, distance, which].astype(jnp.float32) for which in range(1, 5)]
+            grad_query = inverse[:, 0:1] * gain_q * grad[0] - query * cube[:, 0:1]
+            grad_own = inverse[:, 1:2] * gain_k * grad[1] - key * cube[:, 1:2]
+            grad_clean = inverse[:, 2:3] * gain_k * grad[2] - clean_key * cube[:, 2:3]
+            attended_ref[:, cols] = home_ref[head, distance, 0]
+            grads_ref[0, :, cols] = keep * grad_query
+            grads_ref[1, :, cols] = keep * grad_own + grad_clean
+            grads_ref[2, :, cols] = grad[3]
+
+
+def on_group(clean_qkv, noise_qkv, timestep, gain_q, gain_k, attended_grad):
+    rows, local_width = clean_qkv.shape[1:]
+    heads = local_width // GROUP // HEAD_DIM
+    layers = lax.axis_size("tm") // GROUP
+    places = lax.rem(lax.axis_index("tm"), GROUP).astype(jnp.int32)[None]
+    noise_share = noise_share_of(timestep[0])
+    keep_share = 1.0 - noise_share
+    shares = jnp.stack([keep_share, noise_share])
+    gains = jnp.stack([gain_q, gain_k])
+    keep_tile = jnp.full((8, 128), keep_share, jnp.float32)
+
+    smem = pl.BlockSpec(memory_space=pltpu.SMEM)
+    params = pltpu.CompilerParams(vmem_limit_bytes=VMEM_LIMIT)
+    grid = (rows // ROWS,)
+    by_rows = lambda parts: pl.BlockSpec((parts, ROWS, local_width), lambda i: (0, i, 0))
+    flat = lambda count: pl.BlockSpec((ROWS, count), lambda i: (i, 0))
+    by_head = lambda parts: pl.BlockSpec((heads, GROUP, parts, ROWS, HEAD_DIM), lambda i: (0, 0, 0, i, 0))
+    gain_spec = pl.BlockSpec((2, local_width), lambda i: (0, 0))
+    lanes = jax.ShapeDtypeStruct((rows, 128), jnp.float32)
+
+    sums = pl.pallas_call(
+        sums_kernel,
+        grid=grid,
+        in_specs=[smem, by_rows(2), by_rows(2)],
+        out_specs=flat(128),
+        out_shape=lanes,
+        compiler_params=params,
+        name="sums",
+    )(shares, clean_qkv, noise_qkv)
+    sums_other = other_core(sums)
+    packed = pl.pallas_call(
+        functools.partial(pack_kernel, heads),
+        grid=grid,
+        in_specs=[smem, smem, by_rows(3), by_rows(3), flat(local_width), gain_spec, flat(128), flat(128)],
+        out_specs=by_head(6),
+        out_shape=jax.ShapeDtypeStruct((heads, GROUP, 6, rows, HEAD_DIM), jnp.bfloat16),
+        compiler_params=params,
+        name="pack",
+    )(places, shares, clean_qkv, noise_qkv, attended_grad, gains, sums, sums_other)
+
+    half = lambda *lead: pltpu.VMEM(lead + (rows, HEAD_DIM), jnp.bfloat16)
+    full = lambda *lead: pltpu.VMEM(lead + (rows, HEAD_DIM), jnp.float32)
+    copies = lambda *shape: pltpu.SemaphoreType.DMA(shape)
+    home = pl.pallas_call(
+        functools.partial(exchange_kernel, heads, layers),
+        in_specs=[pl.BlockSpec(memory_space=pl.ANY), pl.BlockSpec(memory_space=pltpu.VMEM)],
+        out_specs=pl.BlockSpec(memory_space=pl.ANY),
+        out_shape=jax.ShapeDtypeStruct((heads, GROUP, 5, rows, HEAD_DIM), jnp.bfloat16),
+        scratch_shapes=[
+            half(heads, GROUP, 6),
+            half(heads, GROUP, 2),
+            half(heads, GROUP, 2),
+            half(BACK_SLOTS, GROUP, 5),
+            half(2, GROUP, 2),
+            pltpu.VMEM((GROUP, 8, 128), jnp.float32),
+            half(2 * GROUP),
+            half(2 * GROUP),
+            full(2, 2 * GROUP),
+            full(2, 2 * GROUP),
+            copies(heads),
+            copies(heads, GROUP), copies(heads, GROUP),
+            copies(GROUP), copies(GROUP),
+            copies(heads), copies(heads),
+            copies(heads), copies(heads),
+            copies(heads),
+            copies(heads, GROUP), copies(heads, GROUP),
+            copies(heads),
+            copies(heads, GROUP), copies(heads, GROUP),
+        ],
+        compiler_params=pltpu.CompilerParams(
+            vmem_limit_bytes=EXCHANGE_VMEM, collective_id=0, has_side_effects=True
+        ),
+        cost_estimate=pl.CostEstimate(
+            flops=heads * 2 * 6 * GROUP * (CONTEXT + 1) * rows * rows * HEAD_DIM,
+            bytes_accessed=heads * GROUP * 22 * rows * HEAD_DIM,
+            transcendentals=heads * GROUP * (CONTEXT + 1) * rows * rows,
+        ),
+        name="exchange",
+    )(packed, keep_tile)
+
+    inner = pl.pallas_call(
+        functools.partial(inner_kernel, heads),
+        grid=grid,
+        in_specs=[smem, smem, by_rows(2), by_rows(2), gain_spec, by_head(5)],
+        out_specs=flat(128),
+        out_shape=lanes,
+        compiler_params=params,
+        name="inner",
+    )(places, shares, clean_qkv, noise_qkv, gains, home)
+    inner_other = other_core(inner)
+    attended, clean_grads = pl.pallas_call(
+        functools.partial(finish_kernel, heads),
+        grid=grid,
+        in_specs=[smem, smem, by_rows(2), by_rows(2), gain_spec] + [flat(128)] * 4 + [by_head(5)],
+        out_specs=[flat(local_width), by_rows(3)],
+        out_shape=[
+            jax.ShapeDtypeStruct((rows, local_width), jnp.bfloat16),
+            jax.ShapeDtypeStruct((3, rows, local_width), jnp.float32),
+        ],
+        compiler_params=params,
+        name="finish",
+    )(places, shares, clean_qkv, noise_qkv, gains, sums, sums_other, inner, inner_other, home)
+    return (attended, clean_grads)
+
+
 def solution(mesh):
     placed = (
         P(None, "tm", "head"),
@@ -157,8 +626,10 @@
         P("head"),
         P("tm", "head"),
     )
+    heads_here = D // HEAD_DIM // mesh.shape["head"]
+    grouped = mesh.shape["head"] == 2 and mesh.shape["tm"] % GROUP == 0 and heads_here % GROUP == 0
     return jax.shard_map(
-        on_device,
+        on_group if grouped else on_device,
         mesh=mesh,
         in_specs=placed,
         out_specs=(P("tm", "head"), P(None, "tm", "head")),

time: 1680 us -> 375 us (0.22)
  waiting for transfers between devices: 1090 us -> 2.25 us
  Pallas kernels: 0 us -> 366 us
  matrix products: 307 us -> 0 us
  other arithmetic: 186 us -> 0.1 us
  local copies, waits for them, and re-layouts: 59.8 us -> 0.62 us
    ppermute x6 -> x2, waiting for transfers between devices: 1090 us -> 2.25 us  [other_core(): return lax.ppermute(block, 'head', [(0, 1), (1, 0)])]
    pallas_call x0 -> x5, Pallas kernels: none -> 366 us  [the longest x1 315 us: on_group(): pl.pallas_call(functools.partial(exchange_kernel, heads, layers), in_spec...]
    dot_general x120 -> x0, matrix products: 307 us -> none  [the longest x80 212 us: contract(): lax.dot_general(left, right, (((left_dim,), (right_dim,)), ((), ())), pre...]
    another operation x8 -> x2, other arithmetic: 59.7 us -> 0.1 us  [the longest x1 0.08 us: on_group(): shares = jnp.stack([keep_share, noise_share])]
    convert_element_type x23 -> x0, other arithmetic: 53.3 us -> none  [the longest x20 33.7 us: one_head(): (attention * (grad_probs - row_delta) * score_scale).astype(jnp.bfloat16)]
    another operation x5 -> x2, local copies, waits for them, and re-layouts: 46.1 us -> 0.02 us  [on_group(): gains = jnp.stack([gain_q, gain_k])]
    reduce_sum x23 -> x0, other arithmetic: 33.8 us -> none  [the longest x20 18.9 us: one_head(): row_total = jnp.sum(exponent, axis=-1, keepdims=True)]
    add x2 -> x0, other arithmetic: 29.8 us -> none  [the longest x1 15.6 us: on_device(): context_grads + from_behind(returns_parts[hop_index], 'tm', -(hop_index +...]
  transfers between devices with their start and end apart: 6 -> 2, of which waited for: 5 -> 2; matrix products, arithmetic and copies ran while one was open for 2% -> 0% of each run, Pallas kernels for 0% -> 0%
where the time goes in v2:
time: 375 us; the launch traced here: 373 us
  Pallas kernels  366 us (98%)
    pallas_call x1, Pallas kernels, on_group(): pl.pallas_call(functools.partial(exchange_kernel, heads, layers), in_spec...  315 us
    pallas_call x1, Pallas kernels, on_group(): pl.pallas_call(functools.partial(finish_kernel, heads), grid=grid, in_spe...  17.5 us
    pallas_call x1, Pallas kernels, on_group(): pl.pallas_call(functools.partial(pack_kernel, heads), grid=grid, in_specs...  14.7 us
    pallas_call x1, Pallas kernels, on_group(): pl.pallas_call(functools.partial(inner_kernel, heads), grid=grid, in_spec...  11.4 us
    pallas_call x1, Pallas kernels, on_group(): pl.pallas_call(sums_kernel, grid=grid, in_specs=[smem, by_rows(2), by_row...  7.73 us
  transfers between devices with their start and end apart: 2, of which 2 were waited for; matrix products, arithmetic and copies ran while one was open for 0% of the time, Pallas kernels for 0%

profile of v2, /device:TPU:5, one launch (start us, length us, event | category | flops | bytes accessed | tf_op | source)
XLA Modules:
  0.0 372.7 jit_solution(6085265489864038661)
XLA Ops:
  1.3 0.1 pad_maximum_fusion.1.share_ref
  1.4 0.0 copy-start.1
  1.4 0.0 copy-start.2
  1.4 0.0 copy-start
  1.4 7.7 %sums.1.sums_ref = f32[512,128]{1,0:T(8,128)S(1)} custom-call(f32[2]{0:T(128)S(1)} %pad_maximum_fusion.1.share_ref, bf16[3,512,2560]{2,1,0:T(8,128)(2,1)} %clean_ref.7, bf16[3,512,2560]{2,1,0:T(8,128)(2,1)} %noise_ref.7), custom_call_target="tpu_custom_call" | custom-call | tf_op jit(solution)/shard_map/sums/pallas_call | solution.py:535
  9.1 0.7 collective-permute-start
  9.8 0.0 copy-done.1
  9.9 0.0 copy-done.2
  9.9 1.1 collective-permute-done.other_ref.sums_other_ref
  11.0 0.0 copy-done
  11.0 14.7 %pack.1.packed_ref = bf16[5,4,6,512,128]{4,3,2,1,0:T(8,128)(2,1)} custom-call(s32[1]{0:T(128)} %bitcast.place_ref, f32[2]{0:T(128)S(1)} %pad_maximum_fusion.1.share_ref, bf16[3,512,2560]{2,1,0:T(8,128)(2,1)} %clean_ref.7, bf16[3,512,2560]{2,1,0:T(8,128)(2,1)} %noise_ref.7, bf16[512,2560]{1,0:T(8,128)(2,1)S(1)} %copy-done, ...), custom_call_target="tpu_custom_call" | custom-call | tf_op jit(solution)/shard_map/pack/pallas_call | solution.py:545
  25.7 0.6 broadcast_in_dim.7.keep_ref
  26.3 315.1 %exchange.1.home_ref = bf16[5,4,5,512,128]{4,3,2,1,0:T(8,128)(2,1)} custom-call(bf16[5,4,6,512,128]{4,3,2,1,0:T(8,128)(2,1)} %pack.1.packed_ref, f32[8,128]{1,0:T(8,128)} %broadcast_in_dim.7.keep_ref), custom_call_target="tpu_custom_call" | custom-call | flops 32212254720 | bytes 28835840 | tf_op jit(solution)/shard_map/exchange/pallas_call | solution.py:558
  341.4 11.4 %inner.1.inner_ref = f32[512,128]{1,0:T(8,128)S(1)} custom-call(s32[1]{0:T(128)} %bitcast.place_ref, f32[2]{0:T(128)S(1)} %pad_maximum_fusion.1.share_ref, bf16[3,512,2560]{2,1,0:T(8,128)(2,1)} %clean_ref.7, bf16[3,512,2560]{2,1,0:T(8,128)(2,1)} %noise_ref.7, f32[2,2560]{1,0:T(2,128)S(1)} %pad_maximum_fusion.gains_ref, ...), custom_call_target="tpu_custom_call" | custom-call | tf_op jit(solution)/shard_map/inner/pallas_call | solution.py:595
  352.9 1.1 collective-permute-start.1
  354.0 1.2 collective-permute-done.1.inner_other_ref
  355.2 17.5 %finish.1 = (bf16[512,2560]{1,0:T(8,128)(2,1)}, f32[3,512,2560]{2,1,0:T(8,128)}) custom-call(s32[1]{0:T(128)} %bitcast.place_ref, f32[2]{0:T(128)S(1)} %pad_maximum_fusion.1.share_ref, bf16[3,512,2560]{2,1,0:T(8,128)(2,1)} %clean_ref.7, bf16[3,512,2560]{2,1,0:T(8,128)(2,1)} %noise_ref.7, f32[2,2560]{1,0:T(2,128)S(1)} %pad_maximum_fusion.gains_ref, ...), custom_call_target="tpu_custom_call" | custom-call | tf_op jit(solution)/shard_map/finish/pallas_call | solution.py:605
  (3 shorter events, 0.0 us)
Async XLA Ops:
  1.4 8.5 %copy-start.1 = (f32[2560]{0:T(1024)S(1)}, f32[2560]{0:T(1024)}, u32[]{:S(2)}) copy-start(f32[2560]{0:T(1024)} %param.9) | copy-start | bytes 30724
  1.4 8.5 %copy-start.2 = (f32[2560]{0:T(1024)S(1)}, f32[2560]{0:T(1024)}, u32[]{:S(2)}) copy-start(f32[2560]{0:T(1024)} %param.10) | copy-start | bytes 30724
  1.4 9.6 %copy-start = (bf16[512,2560]{1,0:T(8,128)(2,1)S(1)}, bf16[512,2560]{1,0:T(8,128)(2,1)}, u32[]{:S(2)}) copy-start(bf16[512,2560]{1,0:T(8,128)(2,1)} %grad_ref.1) | copy-start | bytes 7864324
  9.1 1.9 collective-permute-start
  352.9 2.3 collective-permute-start.1

commit v3 on v2

--- a/solution.py
+++ b/solution.py
@@ -174,6 +174,10 @@
     return packed
 
 
+def spread_lanes(packed):
+    return [jnp.broadcast_to(packed[:, index : index + 1], packed.shape) for index in range(3)]
+
+
 def sums_kernel(share_ref, clean_ref, noise_ref, sums_ref):
     keep, share = share_ref[0], share_ref[1]
     clean_key = clean_ref[1].astype(jnp.float32)
@@ -182,10 +186,12 @@
     sums_ref[...] = pack_lanes([jnp.sum(field * field, axis=-1, keepdims=True) for field in (query, key, clean_key)])
 
 
-def pack_kernel(heads, place_ref, share_ref, clean_ref, noise_ref, grad_ref, gains_ref, sums_ref, other_ref, packed_ref):
+def pack_kernel(heads, place_ref, share_ref, clean_ref, noise_ref, grad_ref, gains_ref, sums_ref, other_ref, packed_ref, stats_ref):
     keep, share = share_ref[0], share_ref[1]
     place = place_ref[0]
     inverse = lax.rsqrt((sums_ref[...] + other_ref[...]) / D + epsilon)
+    stats_ref[...] = pack_lanes([keep * inverse[:, 1:2], inverse[:, 2:3], keep])
+    inverse_q, inverse_k, inverse_clean = spread_lanes(inverse)
     for distance in range(GROUP):
         for head in range(heads):
             cols = columns_at(place ^ distance, heads * HEAD_DIM, head * HEAD_DIM, HEAD_DIM)
@@ -196,10 +202,10 @@
             key = keep * clean_key + share * noise_ref[1, :, cols].astype(jnp.float32)
             value = keep * clean_value.astype(jnp.float32) + share * noise_ref[2, :, cols].astype(jnp.float32)
             packed_ref[head, distance, 0] = clean_value
-            packed_ref[head, distance, 1] = (clean_key * inverse[:, 2:3] * gain_k).astype(jnp.bfloat16)
+            packed_ref[head, distance, 1] = (clean_key * inverse_clean * gain_k).astype(jnp.bfloat16)
             packed_ref[head, distance, 2] = value.astype(jnp.bfloat16)
-            packed_ref[head, distance, 3] = (key * inverse[:, 1:2] * gain_k).astype(jnp.bfloat16)
-            packed_ref[head, distance, 4] = (query * inverse[:, 0:1] * gain_q).astype(jnp.bfloat16)
+            packed_ref[head, distance, 3] = (key * inverse_k * gain_k).astype(jnp.bfloat16)
+            packed_ref[head, distance, 4] = (query * inverse_q * gain_q).astype(jnp.bfloat16)
             packed_ref[head, distance, 5] = grad_ref[:, cols]
 
 
@@ -207,9 +213,9 @@
 
 
 def exchange_kernel(
-    heads, layers, packed_ref, keep_ref, home_ref,
-    taken, halo, halo_back, back, halo_out, keeps, keys, values, key_acc, value_acc,
-    own_sem, take_send, take_recv, keep_send, keep_recv, up_send, up_recv, down_send, down_recv,
+    heads, layers, packed_ref, stats_ref, home_ref, inner_ref,
+    taken, halo, halo_back, back, halo_out, stats, keys, values, key_acc, value_acc, own_acc, inner, inner_taken,
+    own_sem, take_send, take_recv, stats_send, stats_recv, inner_send, inner_recv, up_send, up_recv, down_send, down_recv,
     own_back_sem, back_send, back_recv, own_ctx_sem, ctx_send, ctx_recv,
 ):
     tm = lax.axis_index("tm")
@@ -240,8 +246,11 @@
             packed_ref.at[head, d], taken.at[head, d], take_send.at[head, d], take_recv.at[head, d], partner(d)
         )
 
-    def keep_copy(d):
-        return remote(keep_ref, keeps.at[d], keep_send.at[d], keep_recv.at[d], partner(d))
+    def stats_copy(d):
+        return remote(stats_ref, stats.at[d], stats_send.at[d], stats_recv.at[d], partner(d))
+
+    def inner_copy(d):
+        return remote(inner.at[d], inner_taken.at[d], inner_send.at[d], inner_recv.at[d], partner(d))
 
     def up(head):
         return remote(
@@ -255,23 +264,23 @@
 
     def own_back(head):
         return pltpu.make_async_copy(
-            back.at[lax.rem(head, BACK_SLOTS), 0, pl.ds(0, 3)], home_ref.at[head, 0, pl.ds(0, 3)], own_back_sem.at[head]
+            back.at[lax.rem(head, BACK_SLOTS), 0, pl.ds(0, 2)], home_ref.at[head, 0, pl.ds(0, 2)], own_back_sem.at[head]
         )
 
     def give(head, d):
         return remote(
-            back.at[lax.rem(head, BACK_SLOTS), d, pl.ds(0, 3)], home_ref.at[head, d, pl.ds(0, 3)],
+            back.at[lax.rem(head, BACK_SLOTS), d, pl.ds(0, 2)], home_ref.at[head, d, pl.ds(0, 2)],
             back_send.at[head, d], back_recv.at[head, d], partner(d),
         )
 
     def own_ctx(head):
         return pltpu.make_async_copy(
-            back.at[lax.rem(head, BACK_SLOTS), 0, pl.ds(3, 2)], home_ref.at[head, 0, pl.ds(3, 2)], own_ctx_sem.at[head]
+            back.at[lax.rem(head, BACK_SLOTS), 0, pl.ds(2, 2)], home_ref.at[head, 0, pl.ds(2, 2)], own_ctx_sem.at[head]
         )
 
     def give_ctx(head, d):
         return remote(
-            back.at[lax.rem(head, BACK_SLOTS), d, pl.ds(3, 2)], home_ref.at[head, d, pl.ds(3, 2)],
+            back.at[lax.rem(head, BACK_SLOTS), d, pl.ds(2, 2)], home_ref.at[head, d, pl.ds(2, 2)],
             ctx_send.at[head, d], ctx_recv.at[head, d], partner(d),
         )
 
@@ -301,13 +310,19 @@
 
     pl.semaphore_wait(barrier, GROUP - 1 + not_first + not_last)
 
+    start_take(jnp.int32(0))
     for d in range(1, GROUP):
-        keep_copy(d).start()
-    for head in range(min(2, heads)):
-        start_take(jnp.int32(head))
-    keeps[0] = keep_ref[...]
+        stats_copy(d).start()
+    if heads > 1:
+        start_take(jnp.int32(1))
+    stats[0] = stats_ref[...]
+    inner[...] = jnp.zeros_like(inner)
     for d in range(1, GROUP):
-        keep_copy(d).wait_recv()
+        stats_copy(d).wait_recv()
+    lane = lax.broadcasted_iota(jnp.int32, stats.shape[1:], 1)
+
+    def add_inner(d, which, product):
+        inner[d] = inner[d] + jnp.where(lane == which, jnp.sum(product, axis=-1, keepdims=True), 0.0)
 
     def attention(head):
         parity = lax.rem(head, 2)
@@ -344,6 +359,7 @@
             grad_turned = jnp.transpose(grad.astype(jnp.float32))
             delta = jnp.sum(output * grad_turned, axis=0, keepdims=True)
             back[slot_back, d, 0] = jnp.transpose(output).astype(jnp.bfloat16)
+            known = stats[d]
             grad_query = 0.0
             for index in range(CONTEXT + 1):
                 probs = contract(value_blocks[index], grad, 1, 1)
@@ -352,14 +368,17 @@
                 grad_key = jnp.dot(change, query, preferred_element_type=jnp.float32)
                 grad_value = jnp.dot(weights[index], grad, preferred_element_type=jnp.float32)
                 if index == 0:
-                    back[slot_back, d, 2] = grad_key.astype(jnp.bfloat16)
+                    add_inner(d, 1, grad_key * key_blocks[0].astype(jnp.float32))
+                    own_acc[span] = known[:, 0:1] * grad_key
                     own_slot = GROUP + span
-                    value_acc[parity, own_slot] = value_acc[parity, own_slot] + keeps[d, 0:1] * grad_value
+                    value_acc[parity, own_slot] = value_acc[parity, own_slot] + known[:, 2:3] * grad_value
                 else:
                     slot = slots[index - 1]
                     key_acc[parity, slot] = key_acc[parity, slot] + grad_key
                     value_acc[parity, slot] = value_acc[parity, slot] + grad_value
-            back[slot_back, d, 1] = jnp.transpose(grad_query).astype(jnp.bfloat16)
+            grad_query = jnp.transpose(grad_query)
+            add_inner(d, 0, grad_query * query.astype(jnp.float32))
+            back[slot_back, d, 1] = grad_query.astype(jnp.bfloat16)
             return carry
 
         lax.fori_loop(0, GROUP, one_span, 0)
@@ -367,6 +386,9 @@
             spot = across(jnp.int32(distance))
             halo_out[parity, distance, 0] = value_acc[parity, spot].astype(jnp.bfloat16)
             halo_out[parity, distance, 1] = key_acc[parity, spot].astype(jnp.bfloat16)
+            grad_key = key_acc[parity, GROUP + spot]
+            add_inner(distance, 2, grad_key * taken[head, distance, 1].astype(jnp.float32))
+            key_acc[parity, GROUP + spot] = own_acc[spot] + stats[distance][:, 1:2] * grad_key
 
     def step(index, carry):
         @pl.when(index < heads)
@@ -379,9 +401,11 @@
             def _():
                 up(index).start()
 
-            @pl.when(index + 2 < heads)
-            def _():
-                start_take(index + 2)
+            for ahead in (2, 3):
+
+                @pl.when(2 * index + ahead < heads)
+                def _():
+                    start_take(2 * index + ahead)
 
             @pl.when(not_first == 0)
             def _():
@@ -428,10 +452,12 @@
 
             for distance in range(GROUP):
                 spot = GROUP + across(jnp.int32(distance))
-                grad_key = key_acc[parity, spot] + halo_back[head, distance, 1].astype(jnp.float32)
+                later = halo_back[head, distance, 1].astype(jnp.float32)
+                add_inner(distance, 2, later * taken[head, distance, 1].astype(jnp.float32))
+                grad_key = key_acc[parity, spot] + stats[distance][:, 1:2] * later
                 grad_value = value_acc[parity, spot] + halo_back[head, distance, 0].astype(jnp.float32)
-                back[slot_back, distance, 3] = grad_key.astype(jnp.bfloat16)
-                back[slot_back, distance, 4] = grad_value.astype(jnp.bfloat16)
+                back[slot_back, distance, 2] = grad_key.astype(jnp.bfloat16)
+                back[slot_back, distance, 3] = grad_value.astype(jnp.bfloat16)
             own_ctx(head).start()
             for d in range(1, GROUP):
                 give_ctx(head, d).start()
@@ -439,6 +465,8 @@
         return carry
 
     lax.fori_loop(0, heads + 2, step, 0)
+    for d in range(1, GROUP):
+        inner_copy(d).start()
 
     def finish_head(head, carry):
         for d in range(1, GROUP):
@@ -461,30 +489,16 @@
         return carry
 
     lax.fori_loop(0, heads, finish_head, 0)
+    total_inner = inner[0]
     for d in range(1, GROUP):
-        keep_copy(d).wait_send()
+        stats_copy(d).wait_send()
+        inner_copy(d).wait()
+        total_inner = total_inner + inner_taken[d]
+    inner_ref[...] = total_inner
 
 
 def noisy_at(clean_ref, noise_ref, index, cols, keep, share):
     return keep * clean_ref[index, :, cols].astype(jnp.float32) + share * noise_ref[index, :, cols].astype(jnp.float32)
-
-
-def inner_kernel(heads, place_ref, share_ref, clean_ref, noise_ref, gains_ref, home_ref, inner_ref):
-    keep, share = share_ref[0], share_ref[1]
-    place = place_ref[0]
-    inner = [0.0, 0.0, 0.0]
-    for distance in range(GROUP):
-        for head in range(heads):
-            cols = columns_at(place ^ distance, heads * HEAD_DIM, head * HEAD_DIM, HEAD_DIM)
-            gain_q, gain_k = gains_ref[0:1, cols], gains_ref[1:2, cols]
-            terms = (
-                noisy_at(clean_ref, noise_ref, 0, cols, keep, share) * gain_q * home_ref[head, distance, 1].astype(jnp.float32),
-                noisy_at(clean_ref, noise_ref, 1, cols, keep, share) * gain_k * home_ref[head, distance, 2].astype(jnp.float32),
-                clean_ref[1, :, cols].astype(jnp.float32) * gain_k * home_ref[head, distance, 3].astype(jnp.float32),
-            )
-            for index, term in enumerate(terms):
-                inner[index] = inner[index] + term
-    inner_ref[...] = pack_lanes([jnp.sum(part, axis=-1, keepdims=True) for part in inner])
 
 
 def finish_kernel(
@@ -494,7 +508,9 @@
     keep, share = share_ref[0], share_ref[1]
     place = place_ref[0]
     inverse = lax.rsqrt((sums_ref[...] + sums_other_ref[...]) / D + epsilon)
-    cube = inverse * inverse * inverse * ((inner_ref[...] + inner_other_ref[...]) / D)
+    cube = inverse * inverse * ((inner_ref[...] + inner_other_ref[...]) / D)
+    inverse_q = spread_lanes(inverse)[0]
+    cube_q, cube_k, cube_clean = spread_lanes(cube)
     for distance in range(GROUP):
         for head in range(heads):
             cols = columns_at(place ^ distance, heads * HEAD_DIM, head * HEAD_DIM, HEAD_DIM)
@@ -502,14 +518,12 @@
             query = noisy_at(clean_ref, noise_ref, 0, cols, keep, share)
             key = noisy_at(clean_ref, noise_ref, 1, cols, keep, share)
             clean_key = clean_ref[1, :, cols].astype(jnp.float32)
-            grad = [home_ref[head, distance, which].astype(jnp.float32) for which in range(1, 5)]
-            grad_query = inverse[:, 0:1] * gain_q * grad[0] - query * cube[:, 0:1]
-            grad_own = inverse[:, 1:2] * gain_k * grad[1] - key * cube[:, 1:2]
-            grad_clean = inverse[:, 2:3] * gain_k * grad[2] - clean_key * cube[:, 2:3]
+            grad = [home_ref[head, distance, which].astype(jnp.float32) for which in range(1, 4)]
+            grad_query = inverse_q * gain_q * grad[0] - query * cube_q
             attended_ref[:, cols] = home_ref[head, distance, 0]
             grads_ref[0, :, cols] = keep * grad_query
-            grads_ref[1, :, cols] = keep * grad_own + grad_clean
-            grads_ref[2, :, cols] = grad[3]
+            grads_ref[1, :, cols] = gain_k * grad[1] - keep * (key * cube_k) - clean_key * cube_clean
+            grads_ref[2, :, cols] = grad[2]
 
 
 def on_group(clean_qkv, noise_qkv, timestep, gain_q, gain_k, attended_grad):
@@ -521,7 +535,6 @@
     keep_share = 1.0 - noise_share
     shares = jnp.stack([keep_share, noise_share])
     gains = jnp.stack([gain_q, gain_k])
-    keep_tile = jnp.full((8, 128), keep_share, jnp.float32)
 
     smem = pl.BlockSpec(memory_space=pltpu.SMEM)
     params = pltpu.CompilerParams(vmem_limit_bytes=VMEM_LIMIT)
@@ -534,20 +547,20 @@
 
     sums = pl.pallas_call(
         sums_kernel,
-        grid=grid,
-        in_specs=[smem, by_rows(2), by_rows(2)],
-        out_specs=flat(128),
+        grid=(rows // (2 * ROWS),),
+        in_specs=[smem] + [pl.BlockSpec((2, 2 * ROWS, local_width), lambda i: (0, i, 0))] * 2,
+        out_specs=pl.BlockSpec((2 * ROWS, 128), lambda i: (i, 0)),
         out_shape=lanes,
         compiler_params=params,
         name="sums",
     )(shares, clean_qkv, noise_qkv)
     sums_other = other_core(sums)
-    packed = pl.pallas_call(
+    packed, stats = pl.pallas_call(
         functools.partial(pack_kernel, heads),
         grid=grid,
         in_specs=[smem, smem, by_rows(3), by_rows(3), flat(local_width), gain_spec, flat(128), flat(128)],
-        out_specs=by_head(6),
-        out_shape=jax.ShapeDtypeStruct((heads, GROUP, 6, rows, HEAD_DIM), jnp.bfloat16),
+        out_specs=[by_head(6), flat(128)],
+        out_shape=[jax.ShapeDtypeStruct((heads, GROUP, 6, rows, HEAD_DIM), jnp.bfloat16), lanes],
         compiler_params=params,
         name="pack",
     )(places, shares, clean_qkv, noise_qkv, attended_grad, gains, sums, sums_other)
@@ -555,24 +568,28 @@
     half = lambda *lead: pltpu.VMEM(lead + (rows, HEAD_DIM), jnp.bfloat16)
     full = lambda *lead: pltpu.VMEM(lead + (rows, HEAD_DIM), jnp.float32)
     copies = lambda *shape: pltpu.SemaphoreType.DMA(shape)
-    home = pl.pallas_call(
+    home, inner = pl.pallas_call(
         functools.partial(exchange_kernel, heads, layers),
         in_specs=[pl.BlockSpec(memory_space=pl.ANY), pl.BlockSpec(memory_space=pltpu.VMEM)],
-        out_specs=pl.BlockSpec(memory_space=pl.ANY),
-        out_shape=jax.ShapeDtypeStruct((heads, GROUP, 5, rows, HEAD_DIM), jnp.bfloat16),
+        out_specs=[pl.BlockSpec(memory_space=pl.ANY), pl.BlockSpec(memory_space=pltpu.VMEM)],
+        out_shape=[jax.ShapeDtypeStruct((heads, GROUP, 4, rows, HEAD_DIM), jnp.bfloat16), lanes],
         scratch_shapes=[
             half(heads, GROUP, 6),
             half(heads, GROUP, 2),
             half(heads, GROUP, 2),
-            half(BACK_SLOTS, GROUP, 5),
+            half(BACK_SLOTS, GROUP, 4),
             half(2, GROUP, 2),
-            pltpu.VMEM((GROUP, 8, 128), jnp.float32),
+            full(GROUP),
             half(2 * GROUP),
             half(2 * GROUP),
             full(2, 2 * GROUP),
             full(2, 2 * GROUP),
+            full(GROUP),
+            full(GROUP),
+            full(GROUP),
             copies(heads),
             copies(heads, GROUP), copies(heads, GROUP),
+            copies(GROUP), copies(GROUP),
             copies(GROUP), copies(GROUP),
             copies(heads), copies(heads),
             copies(heads), copies(heads),
@@ -590,22 +607,13 @@
             transcendentals=heads * GROUP * (CONTEXT + 1) * rows * rows,
         ),
         name="exchange",
-    )(packed, keep_tile)
-
-    inner = pl.pallas_call(
-        functools.partial(inner_kernel, heads),
-        grid=grid,
-        in_specs=[smem, smem, by_rows(2), by_rows(2), gain_spec, by_head(5)],
-        out_specs=flat(128),
-        out_shape=lanes,
-        compiler_params=params,
-        name="inner",
-    )(places, shares, clean_qkv, noise_qkv, gains, home)
+    )(packed, stats)
+
     inner_other = other_core(inner)
     attended, clean_grads = pl.pallas_call(
         functools.partial(finish_kernel, heads),
         grid=grid,
-        in_specs=[smem, smem, by_rows(2), by_rows(2), gain_spec] + [flat(128)] * 4 + [by_head(5)],
+        in_specs=[smem, smem, by_rows(2), by_rows(2), gain_spec] + [flat(128)] * 4 + [by_head(4)],
         out_specs=[flat(local_width), by_rows(3)],
         out_shape=[
             jax.ShapeDtypeStruct((rows, local_width), jnp.bfloat16),

time: 375 us -> 358 us (0.955)
  Pallas kernels: 366 us -> 348 us
    pallas_call x2 -> x1, Pallas kernels: 19.2 us -> 6.09 us  [on_group(): pl.pallas_call(sums_kernel, grid=(rows // (2 * ROWS),), in_specs=[smem] +...]
    pallas_call x1, Pallas kernels: 315 us -> 310 us  [on_group(): pl.pallas_call(functools.partial(exchange_kernel, heads, layers), in_spec...]
where the time goes in v3:
time: 358 us; the launch traced here: 355 us
  Pallas kernels  348 us (97%)
    pallas_call x1, Pallas kernels, on_group(): pl.pallas_call(functools.partial(exchange_kernel, heads, layers), in_spec...  310 us
    pallas_call x1, Pallas kernels, on_group(): pl.pallas_call(functools.partial(finish_kernel, heads), grid=grid, in_spe...  16.4 us
    pallas_call x1, Pallas kernels, on_group(): pl.pallas_call(functools.partial(pack_kernel, heads), grid=grid, in_specs...  14.7 us
  transfers between devices with their start and end apart: 2, of which 2 were waited for; matrix products, arithmetic and copies ran while one was open for 0% of the time, Pallas kernels for 0%

profile of v3, /device:TPU:5, one launch (start us, length us, event | category | flops | bytes accessed | tf_op | source)
XLA Modules:
  0.0 355.2 jit_solution(13463783865971667017)
XLA Ops:
  1.3 0.1 pad_maximum_fusion.1.share_ref
  1.4 0.0 copy-start.3
  1.4 0.0 copy-start.4
  1.4 0.0 copy-start
  1.4 6.1 %sums.1.sums_ref = f32[512,128]{1,0:T(8,128)S(1)} custom-call(f32[2]{0:T(128)S(1)} %pad_maximum_fusion.1.share_ref, bf16[3,512,2560]{2,1,0:T(8,128)(2,1)} %clean_ref.5, bf16[3,512,2560]{2,1,0:T(8,128)(2,1)} %noise_ref.5), custom_call_target="tpu_custom_call" | custom-call | tf_op jit(solution)/shard_map/sums/pallas_call | solution.py:548
  7.5 0.7 collective-permute-start
  8.2 0.0 copy-done.3
  8.3 0.0 copy-done.4
  8.3 1.1 collective-permute-done.other_ref.sums_other_ref
  9.4 0.0 copy-done
  9.4 14.7 %pack.1 = (bf16[5,4,6,512,128]{4,3,2,1,0:T(8,128)(2,1)}, f32[512,128]{1,0:T(8,128)S(1)}) custom-call(s32[1]{0:T(128)} %bitcast.place_ref, f32[2]{0:T(128)S(1)} %pad_maximum_fusion.1.share_ref, bf16[3,512,2560]{2,1,0:T(8,128)(2,1)} %clean_ref.5, bf16[3,512,2560]{2,1,0:T(8,128)(2,1)} %noise_ref.5, bf16[512,2560]{1,0:T(8,128)(2,1)S(1)} %copy-done, ...), custom_call_target="tpu_custom_call" | custom-call | tf_op jit(solution)/shard_map/pack/pallas_call | solution.py:558
  24.1 0.0 copy-start.2
  24.1 0.7 copy-done.2
  24.8 310.4 %exchange.1 = (bf16[5,4,4,512,128]{4,3,2,1,0:T(8,128)(2,1)}, f32[512,128]{1,0:T(8,128)}) custom-call(bf16[5,4,6,512,128]{4,3,2,1,0:T(8,128)(2,1)} %get-tuple-element.6.packed_ref, f32[512,128]{1,0:T(8,128)} %copy-done.2), custom_call_target="tpu_custom_call" | custom-call | flops 32212254720 | bytes 28835840 | tf_op jit(solution)/shard_map/exchange/pallas_call | solution.py:571
  335.2 1.3 collective-permute-start.1
  336.4 1.4 collective-permute-done.1.inner_other_ref
  337.8 0.0 copy-start.1
  337.8 0.9 copy-done.1
  338.8 16.4 %finish.1 = (bf16[512,2560]{1,0:T(8,128)(2,1)}, f32[3,512,2560]{2,1,0:T(8,128)}) custom-call(s32[1]{0:T(128)} %bitcast.place_ref, f32[2]{0:T(128)S(1)} %pad_maximum_fusion.1.share_ref, bf16[3,512,2560]{2,1,0:T(8,128)(2,1)} %clean_ref.5, bf16[3,512,2560]{2,1,0:T(8,128)(2,1)} %noise_ref.5, f32[2,2560]{1,0:T(2,128)S(1)} %pad_maximum_fusion.gains_ref, ...), custom_call_target="tpu_custom_call" | custom-call | tf_op jit(solution)/shard_map/finish/pallas_call | solution.py:613
  (3 shorter events, 0.0 us)
Async XLA Ops:
  1.4 6.8 %copy-start.3 = (f32[2560]{0:T(1024)S(1)}, f32[2560]{0:T(1024)}, u32[]{:S(2)}) copy-start(f32[2560]{0:T(1024)} %param.9) | copy-start | bytes 30724
  1.4 6.9 %copy-start.4 = (f32[2560]{0:T(1024)S(1)}, f32[2560]{0:T(1024)}, u32[]{:S(2)}) copy-start(f32[2560]{0:T(1024)} %param.10) | copy-start | bytes 30724
  1.4 8.0 %copy-start = (bf16[512,2560]{1,0:T(8,128)(2,1)S(1)}, bf16[512,2560]{1,0:T(8,128)(2,1)}, u32[]{:S(2)}) copy-start(bf16[512,2560]{1,0:T(8,128)(2,1)} %grad_ref.1) | copy-start | bytes 7864324
  7.5 1.9 collective-permute-start
  24.1 0.7 copy-start.2
  335.2 2.6 collective-permute-start.1
  337.8 0.9 copy-start.1
